TPU v7x, 128 devices: a whole 4x4x4 slice. The times are simulated.
128 devices in a mesh: mem: 8 (over z_lo, x), tile: 16 (over y, z_hi, core).
Axes of the slice: x: 4, y: 4, z: 4 (z_hi: 2, z_lo: 2; z = z_hi * 2 + z_lo), core: 2. Of those that a mesh axis runs over, the one named last changes fastest.
Arguments:
- alpha: bfloat16 [80, 8, 512, 384], P('mem', None, 'tile'), may hold values from -6 to 6
- perturbation: bfloat16 [80, 8, 512, 384], P('mem', None, 'tile'), may hold values from -6 to 6
- cotangent: bfloat16 [8, 786432], P('mem', 'tile'), may hold values from -6 to 6
- decay_y: float32 [8, 512], P(None, 'tile'), may hold values from 0.4 to 1
- decay_x: float32 [8, 384], replicated, may hold values from 0.4 to 1
- group_members: int32 [8], replicated, may hold values from 2 to 10, as said below
- interp_weight: bfloat16 [16, 16, 128, 32, 128], P('tile'), may hold values from -0.5 to 0.5
- pair_count: int32 [16, 16], replicated, may hold values from 0 to 128, as said below
- src_index: int32 [16, 16, 128], replicated, may hold values from 0 to 383
- dst_index: int32 [16, 16, 128], replicated, may hold values from 0 to 383
Outputs:
- increment: float32 [8, 786432], P('mem', 'tile')
- alpha_grad: float32 [80, 8, 512, 384], P('mem', None, 'tile')
Inputs may be any that keep to these rules, and one draw needn't show every extreme that they name: Slots 0 to group_members[g] - 1 of group g hold live members; some group holds 10. `pair_count`: one destination tile has 128 live slots from every source tile.
All inputs are finite; a program needn't handle non-finite values.
Results may differ from a plain program's by a relative error of at most 0.0029.
Values may be sent and summed in bfloat16 or wider, within the bound.
A program may use at most 128 MiB of HBM per device.

v0:
```python
import jax
import jax.numpy as jnp
from jax import lax
from jax.sharding import PartitionSpec as P


def entering(part, axis, combine, identity, reverse):
    count = lax.axis_size(axis)
    place = lax.axis_index(axis)
    ahead = count - 1 - place if reverse else place
    gathered = jax.tree.map(lambda a: lax.all_gather(a, axis), part)
    state = jax.tree.map(lambda a, e: jnp.zeros_like(a) + jnp.asarray(e, a.dtype), part, identity)

    def one(lap, state):
        source = count - 1 - lap if reverse else lap
        return combine(
            state, jax.tree.map(lambda a: lax.dynamic_index_in_dim(a, source, 0, False), gathered)
        )

    return lax.fori_loop(0, ahead, one, state)


def coefficient(decay):
    return ((1.0 - decay * decay) ** 3 / (1.0 + decay * decay)) ** 0.25


def filter_tables(decay):
    scaling = coefficient(decay)
    logarithm_sums = jnp.cumsum(jnp.log(decay), axis=1)
    log_gaps = logarithm_sums[:, :, None] - logarithm_sums[:, None, :]
    row_index = jnp.arange(decay.shape[1])
    lower_part = row_index[:, None] >= row_index[None, :]
    upper_part = row_index[:, None] <= row_index[None, :]
    down_matrix = (
        jnp.where(lower_part, jnp.exp(jnp.where(lower_part, log_gaps, 0.0)), 0.0)
        * scaling[:, None, :]
    )
    up_matrix = jnp.where(upper_part, jnp.exp(jnp.where(upper_part, -log_gaps, 0.0)), 0.0)
    return (scaling, logarithm_sums, down_matrix, up_matrix)


def column_matrix(decay_x):
    scaling, logarithm_sums, down_matrix, up_matrix = filter_tables(decay_x)
    return jnp.einsum("lmi,lmj->lij", down_matrix, down_matrix, precision=lax.Precision.HIGHEST)


def filter_columns(values, column_filter):
    return jnp.einsum("slyj,lij->slyi", values, column_filter, precision=lax.Precision.HIGHEST)


def combine_steps(earlier_step, later_step):
    early_rate, leading_sum = earlier_step
    late_rate, late_sum = later_step
    return (early_rate * late_rate, late_rate[None, :, None] * leading_sum + late_sum)


def filter_rows(values, decay_y):
    scaling, logarithm_sums, down_matrix, up_matrix = filter_tables(decay_y)
    product_all = jnp.exp(logarithm_sums[:, -1])
    local_down = jnp.einsum("lij,sljx->slix", down_matrix, values, precision=lax.Precision.HIGHEST)
    neutral = (jnp.ones_like(product_all), jnp.zeros_like(local_down[:, :, 0, :]))
    carry_down = entering(
        (product_all, local_down[:, :, -1, :]), "tile", combine_steps, neutral, False
    )[1]
    smooth = local_down + jnp.exp(logarithm_sums)[None, :, :, None] * carry_down[:, :, None, :]
    local_up = jnp.einsum("lim,slmx->slix", up_matrix, smooth, precision=lax.Precision.HIGHEST)
    initial_damping = decay_y[:, 0]
    carry_up = entering(
        (product_all, initial_damping[None, :, None] * local_up[:, :, 0, :]),
        "tile",
        combine_steps,
        neutral,
        True,
    )[1]
    tail_decay = jnp.exp(logarithm_sums[:, -1:] - logarithm_sums)
    return scaling[None, :, :, None] * (
        local_up + tail_decay[None, :, :, None] * carry_up[:, :, None, :]
    )


def shards(
    alpha,
    perturbation,
    cotangent,
    decay_y,
    decay_x,
    group_members,
    interp_weight,
    pair_count,
    src_index,
    dst_index,
):
    members = alpha.shape[0]
    rows_dev = alpha.shape[2]
    columns = alpha.shape[3]
    levels_dev = cotangent.shape[0]
    slots_pair = interp_weight.shape[2]
    block_src = interp_weight.shape[3]
    block_dst = interp_weight.shape[4]
    blocks_src = rows_dev * columns // block_src
    blocks_dst = cotangent.shape[1] // block_dst
    tile_count = lax.axis_size("tile")
    group_index = lax.axis_index("mem")
    tile_index = lax.axis_index("tile")
    own_count = lax.dynamic_index_in_dim(group_members, group_index, 0, keepdims=False)
    live_slots = (jnp.arange(members) < own_count).astype(jnp.float32)
    member_scale = 1.0 / jnp.sqrt(jnp.sum(group_members).astype(jnp.float32) - 1.0)
    column_filter = column_matrix(decay_x)
    smooth = filter_columns(filter_rows(alpha.astype(jnp.float32), decay_y), column_filter)
    partial_value = jnp.sum(
        live_slots[:, None, None, None] * perturbation.astype(jnp.float32) * smooth, axis=0
    )
    level_total = lax.psum(partial_value, "mem")
    level_share = lax.dynamic_slice_in_dim(level_total, group_index * levels_dev, levels_dev, 0)
    low_values = (level_share * member_scale).astype(jnp.bfloat16)
    low_blocks = jnp.transpose(low_values.reshape(levels_dev, blocks_src, block_src), (1, 0, 2))
    weights = interp_weight[0]
    counts_row = lax.dynamic_index_in_dim(pair_count, tile_index, 0, keepdims=False)
    slot_mask = (jnp.arange(slots_pair)[None, :] < counts_row[:, None]).astype(jnp.float32)
    source_rows = lax.dynamic_index_in_dim(src_index, tile_index, 0, keepdims=False)
    target_rows = lax.dynamic_index_in_dim(dst_index, tile_index, 0, keepdims=False)
    offsets = (jnp.arange(tile_count, dtype=jnp.int32) * blocks_src)[:, None]
    every_tile = lax.all_gather(low_blocks, "tile", axis=0, tiled=True)
    picked = every_tile[offsets + source_rows]
    contrib = jnp.einsum("sclb,scbe->scle", picked, weights, preferred_element_type=jnp.float32)
    contrib = contrib * slot_mask[:, :, None, None]
    summed = jax.ops.segment_sum(
        contrib.reshape(-1, levels_dev, block_dst), target_rows.reshape(-1), num_segments=blocks_dst
    )
    increment = jnp.transpose(summed, (1, 0, 2)).reshape(levels_dev, blocks_dst * block_dst)
    grad_blocks = jnp.transpose(cotangent.reshape(levels_dev, blocks_dst, block_dst), (1, 0, 2))[
        target_rows
    ]
    back_terms = jnp.einsum(
        "scle,scbe->sclb", grad_blocks, weights, preferred_element_type=jnp.float32
    )
    back_terms = back_terms * slot_mask[:, :, None, None]
    spread = jax.ops.segment_sum(
        back_terms.reshape(-1, levels_dev, block_src),
        (offsets + source_rows).reshape(-1),
        num_segments=tile_count * blocks_src,
    )
    back_share = lax.psum_scatter(spread, "tile", scatter_dimension=0, tiled=True)
    back_field = jnp.transpose(back_share, (1, 0, 2)).reshape(levels_dev, rows_dev, columns)
    all_levels = lax.all_gather(back_field, "mem", axis=0, tiled=True)
    weighted = perturbation.astype(jnp.float32) * all_levels[None]
    smooth_back = filter_rows(filter_columns(weighted, column_filter), decay_y)
    alpha_grad = (live_slots * member_scale)[:, None, None, None] * smooth_back
    return (increment, alpha_grad)


def solution(mesh):
    in_specs = (
        P("mem", None, "tile", None),
        P("mem", None, "tile", None),
        P("mem", "tile"),
        P(None, "tile"),
        P(),
        P(),
        P("tile", None, None, None, None),
        P(),
        P(),
        P(),
    )
    out_specs = (P("mem", "tile"), P("mem", None, "tile", None))
    return jax.shard_map(shards, mesh=mesh, in_specs=in_specs, out_specs=out_specs, check_vma=False)
```

profile of v0, /device:TPU:1, one launch (start us, length us, event | category | flops | bytes accessed | tf_op | source)
XLA Modules:
  0.0 516.4 jit_solution(14088290818294802280)
XLA Ops:
  8.1 1.5 reduce.4
  10.4 6.2 %gather_fusion.1 = bf16[2048,128]{1,0:T(8,128)(2,1)S(1)} fusion(bf16[384,128]{1,0:T(8,128)(2,1)S(1)} %bitcast.125, s32[2048]{0:T(1024)S(1)} %get-tuple-element.352), kind=kCustom, calls=%fused_computation.1 | custom fusion | bytes 1056768 | tf_op jit(solution)/shard_map/gather | solution.py:131
  16.6 12.2 %fusion = f32[16,128,1,32]{3,2,1,0:T(1,128)S(1)} fusion(bf16[1,16,128,32,128]{4,3,2,1,0:T(8,128)(2,1)} %param.24, bf16[16,128,128,1]{2,1,0,3:T(8,128)(2,1)S(1)} %bitcast.134), kind=kOutput, calls=%fused_computation.12 | convolution fusion | flops 16777216 | bytes 17563648 | tf_op jit(solution)/shard_map/scle,scbe->sclb/dot_general | solution.py:134
  29.3 13.3 %scatter_custom_fusion.1 = f32[6144,32]{1,0:T(8,128)} fusion(s32[2048]{0:T(1024)S(1)} %bitcast.139, f32[2048,32]{1,0:T(8,128)S(1)} %bitcast.130, f32[]{:T(128)} %constant.132.clone.1), kind=kCustom, calls=%fused_computation.61 | custom fusion | flops 65536 | bytes 786436 | tf_op jit(solution)/shard_map/scatter-add | solution.py:138
  42.9 1.8 convolution_bitcast_fusion
  44.7 1.9 copy-done.5
  49.0 13.0 %fusion.8 = f32[8,384,384]{2,1,0:T(8,128)} fusion(f32[8,384]{1,0:T(8,128)S(1)} %get-tuple-element.345, f32[8,384]{1,0:T(8,128)S(1)} %add_bitcast_fusion, pred[384,384]{0,1:T(8,128)(4,1)S(1)} %iota_compare_fusion), kind=kOutput, calls=%fused_computation.22 | convolution fusion | flops 5440536576 | bytes 4890624 | tf_op jit(solution)/shard_map/lmi,lmj->lij/dot_general | solution.py:44
  62.0 58.2 %reduce-scatter.2.cloned.1.call-done = f32[384,1,32]{2,0,1:T(8,128)} async-done(((f32[6144,1,32]{2,0,1:T(8,128)}), f32[384,1,32]{2,0,1:T(8,128)}) %reduce-scatter.2.cloned.1.call-update) | async-done | bytes 49168 | tf_op jit(solution)/shard_map/reduce_scatter | solution.py:143
  121.2 23.5 %all_gather.34 = f32[8,32,384]{2,1,0:T(8,128)S(1)} all-gather(f32[1,32,384]{2,1,0:T(8,128)S(1)} %reshape_transpose.7), channel_id=1, replica_groups=mesh['mem'=8,'tile'=16] {'mem'}, dimensions={0}, use_global_device_ids=true | all-gather | bytes 442368 | tf_op jit(solution)/shard_map/all_gather | solution.py:145
  144.7 9.8 %fusion.4 = f32[8,384,10,32]{1,3,2,0:T(8,128)S(1)} fusion(f32[8,384,384]{2,1,0:T(8,128)} %fusion.8, f32[8,32,384]{2,1,0:T(8,128)S(1)} %all_gather.34, bf16[10,8,32,384]{3,2,1,0:T(8,128)(2,1)S(1)} %copy-done.6), kind=kOutput, calls=%fused_computation.18 | convolution fusion | flops 4531814400 | bytes 11010048 | tf_op jit(solution)/shard_map/slyj,lij->slyi/dot_general | solution.py:48
  154.5 3.6 fusion.38
  158.0 1.9 copy-done.4
  162.4 40.0 %all-reduce = f32[128]{0:T(128)S(1)} all-reduce(f32[128]{0:T(128)S(1)} %dynamic-update-slice), channel_id=2, replica_groups=mesh['mem'=8,'tile'=16] {'tile'}, use_global_device_ids=true, to_apply=%add | all-reduce | flops 128 | bytes 1024
  202.7 4.0 copy.54
  208.0 5.9 %fusion.32 = f32[10,8,32,384]{3,2,0,1:T(8,128)S(1)} fusion(f32[10,8,32,384]{3,2,0,1:T(8,128)} %copy-done.5, f32[10,8,384]{2,0,1:T(8,128)S(1)} %copy.55, f32[8,32]{1,0:T(8,128)S(1)} %get-tuple-element.347, f32[8,32]{1,0:T(8,128)S(1)} %reduce_window_sum.36, pred[32,32]{1,0:T(8,128)(4,1)S(1)} %iota_compare_fusion.1), kind=kOutput, calls=%fused_computation.47 | convolution fusion | flops 379486208 | bytes 7990272 | tf_op jit(solution)/shard_map/lim,slmx->slix/dot_general | solution.py:66
  214.0 1.9 copy-done.3
  216.0 5.2 %all-gather.14.cloned.1.call-done = f32[160,8,1,384]{3,2,0,1:T(1,128)} async-done(((f32[10,8,1,384]{3,2,0,1:T(1,128)}), f32[160,8,1,384]{3,2,0,1:T(1,128)}) %all-gather.14.cloned.1.call-update) | async-done | bytes 1966096 | tf_op jit(solution)/shard_map/all_gather | solution.py:11
  221.2 3.9 copy.58
  226.3 5.9 %fusion.35 = f32[10,8,32,384]{3,2,0,1:T(8,128)S(1)} fusion(f32[10,8,32,384]{3,2,0,1:T(8,128)} %copy-done.4, f32[10,8,384]{2,0,1:T(8,128)S(1)} %copy.59, f32[8,32]{1,0:T(8,128)S(1)} %get-tuple-element.347, f32[8,32]{1,0:T(8,128)S(1)} %reduce_window_sum.36, pred[32,32]{1,0:T(8,128)(4,1)S(1)} %iota_compare_fusion.1), kind=kOutput, calls=%fused_computation.48 | convolution fusion | flops 379486208 | bytes 7990272 | tf_op jit(solution)/shard_map/lim,slmx->slix/dot_general | solution.py:66
  232.2 1.9 copy-done.2
  239.4 63.1 %all-gather.10.cloned.1.call-done = f32[16,10,8,384]{3,2,1,0:T(8,128)} async-done(((f32[1,10,8,384]{3,2,1,0:T(8,128)}), f32[16,10,8,384]{3,2,1,0:T(8,128)}) %all-gather.10.cloned.1.call-update) | async-done | bytes 1966096 | tf_op jit(solution)/shard_map/all_gather | solution.py:11
  302.5 14.6 %while.55 = (s32[]{:T(128)}, f32[10,8,384]{2,1,0:T(8,128)S(1)}, s32[]{:T(128)}, f32[16,8]{1,0:T(8,128)S(1)}, f32[16,10,8,384]{3,2,1,0:T(8,128)}, /*index=5*/s32[]{:T(128)}, s32[]{:T(128)}, s32[]{:T(128)}, s32[]{:T(128)}) while((s32[]{:T(128)}, f32[10,8,384]{2,1,0:T(8,128)S(1)}, s32[]{:T(128)}, f32[16,8]{1,0:T(8,128)S(1)}, ...), condition=%wide.region_16.17_spmd, body=%wide.region_15.16_spmd.sunk | while | flops 61446 | bytes 368883 | solution.py:20
  317.1 34.4 %all-gather.8.cloned.1.call-done = f32[16,10,8,384]{3,2,1,0:T(8,128)} async-done(((f32[1,10,8,384]{3,2,1,0:T(8,128)}), f32[16,10,8,384]{3,2,1,0:T(8,128)}) %all-gather.8.cloned.1.call-update) | async-done | bytes 1966096 | tf_op jit(solution)/shard_map/all_gather | solution.py:11
  351.6 14.8 %while.53 = (s32[]{:T(128)}, f32[10,8,384]{2,1,0:T(8,128)S(1)}, s32[]{:T(128)}, f32[16,8]{1,0:T(8,128)S(1)}, f32[16,10,8,384]{3,2,1,0:T(8,128)}, /*index=5*/s32[]{:T(128)}, s32[]{:T(128)}, s32[]{:T(128)}, s32[]{:T(128)}) while((s32[]{:T(128)}, f32[10,8,384]{2,1,0:T(8,128)S(1)}, s32[]{:T(128)}, f32[16,8]{1,0:T(8,128)S(1)}, ...), condition=%wide.region_6.7_spmd, body=%wide.region_5.6_spmd.sunk | while | flops 61446 | bytes 368883 | solution.py:20
  366.4 14.7 %fusion.15 = f32[8,32,384]{2,1,0:T(8,128)} fusion(f32[10]{0:T(128)S(1)} %compare_convert_fusion, bf16[10,8,32,384]{3,2,1,0:T(8,128)(2,1)S(1)} %copy-done.6, f32[10,8,32,384]{3,2,0,1:T(8,128)} %copy-done.3, f32[10,8,384]{2,0,1:T(8,128)S(1)} %copy.57, f32[8,32]{1,0:T(8,128)S(1)} %get-tuple-element.346, f32[8,32]{1,0:T(8,128)S(1)} %get-tuple-element.349, ...), kind=kOutput, calls=%fused_computation.29 | convolution fusion | flops 4536631296 | bytes 11135016 | tf_op jit(solution)/shard_map/slyj,lij->slyi/dot_general | solution.py:48
  381.1 2.9 multiply_multiply_fusion
  384.1 2.3 copy.62
  386.4 61.3 %all-reduce.3.cloned.1.call-done = f32[8,32,384]{2,1,0:T(8,128)} async-done(((f32[8,32,384]{2,1,0:T(8,128)}), f32[8,32,384]{2,1,0:T(8,128)}) %all-reduce.3.cloned.1.call-update) | async-done | bytes 393232 | tf_op jit(solution)/shard_map/psum | solution.py:113
  448.6 33.9 %all_gather.33 = bf16[6144,1,32]{2,0,1:T(8,128)(2,1)S(1)} all-gather(bf16[384,1,32]{2,0,1:T(8,128)(2,1)S(1)} %transpose_reshape.6), channel_id=1, replica_groups=mesh['mem'=8,'tile'=16] {'tile'}, dimensions={0}, use_global_device_ids=true | all-gather | bytes 417792 | tf_op jit(solution)/shard_map/all_gather | solution.py:123
  482.5 6.2 %gather_fusion = bf16[2048,32]{1,0:T(8,128)(2,1)S(1)} fusion(bf16[6144,32]{1,0:T(8,128)(2,1)S(1)} %bitcast.126, s32[2048]{0:T(1024)S(1)} %get-tuple-element.342), kind=kCustom, calls=%fused_computation | custom fusion | bytes 270336 | tf_op jit(solution)/shard_map/gather | solution.py:124
  488.7 8.2 %fusion.2 = f32[16,128,1,128]{3,2,1,0:T(1,128)S(1)} fusion(bf16[1,16,128,32,128]{4,3,2,1,0:T(8,128)(2,1)} %param.24, bf16[16,128,32,1]{2,1,0,3:T(8,128)(2,1)S(1)} %bitcast.135), kind=kOutput, calls=%fused_computation.14 | convolution fusion | flops 16777216 | bytes 17956864 | tf_op jit(solution)/shard_map/sclb,scbe->scle/dot_general | solution.py:125
  497.2 12.1 %scatter_custom_fusion = f32[384,128]{1,0:T(8,128)} fusion(s32[2048]{0:T(1024)S(1)} %dynamic-slice_bitcast_fusion.4, f32[2048,128]{1,0:T(8,128)S(1)} %bitcast.131, f32[]{:T(128)} %constant.132.clone.1), kind=kCustom, calls=%fused_computation.80 | custom fusion | flops 262144 | bytes 196612 | tf_op jit(solution)/shard_map/scatter-add | solution.py:127
  (139 shorter events, 46.6 us)
Async XLA Ops:
  7.2 35.7 %copy-start = (bf16[10,8,32,384]{3,2,1,0:T(8,128)(2,1)S(1)}, bf16[10,8,32,384]{3,2,1,0:T(8,128)(2,1)}, u32[]{:S(2)}) copy-start(bf16[10,8,32,384]{3,2,1,0:T(8,128)(2,1)} %param.18) | copy-start | bytes 5898244
  7.2 112.9 %reduce-scatter.2.cloned.1.call-start = ((), (), s32[]{:S(2)}) async-start(), calls=%async_computation.3 | async-start | bytes 3342336 | tf_op jit(solution)/shard_map/reduce_scatter | solution.py:143
  28.8 13.8 %copy-start.7 = (f32[8,32]{1,0:T(8,128)S(1)}, f32[8,32]{1,0:T(8,128)}, u32[]{:S(2)}) copy-start(f32[8,32]{1,0:T(8,128)} %param.21) | copy-start | bytes 3076
  42.6 5.2 %copy-start.8 = (f32[8,384]{1,0:T(8,128)S(1)}, f32[8,384]{1,0:T(8,128)}, u32[]{:S(2)}) copy-start(f32[8,384]{1,0:T(8,128)} %param.22) | copy-start | bytes 36868
  42.6 160.1 %all-gather.12.cloned.1.call-start = ((), (), s32[]{:S(2)}) async-start(), calls=%async_computation.5 | async-start | bytes 2088960 | tf_op jit(solution)/shard_map/all_gather | solution.py:11
  44.7 1.9 copy-start.5
  47.4 173.8 %all-gather.14.cloned.1.call-start = ((), (), s32[]{:S(2)}) async-start(), calls=%async_computation.6 | async-start | bytes 2088960 | tf_op jit(solution)/shard_map/all_gather | solution.py:11
  49.0 95.7 %copy-start.6 = (bf16[10,8,32,384]{3,2,1,0:T(8,128)(2,1)S(1)}, bf16[10,8,32,384]{3,2,1,0:T(8,128)(2,1)}, u32[]{:S(2)}) copy-start(bf16[10,8,32,384]{3,2,1,0:T(8,128)(2,1)} %param.19) | copy-start | bytes 5898244
  154.4 6.3 %copy-start.10 = (u32[128]{0:T(128)S(1)}, u32[128]{0:T(128)}, u32[]{:S(2)}) copy-start(u32[128]{0:T(128)} %constant.151) | copy-start | bytes 1540
  158.0 1.9 copy-start.4
  160.7 141.8 %all-gather.10.cloned.1.call-start = ((), (), s32[]{:S(2)}) async-start(), calls=%async_computation.4 | async-start | bytes 2088960 | tf_op jit(solution)/shard_map/all_gather | solution.py:11
  214.0 1.9 copy-start.3
  226.3 9.4 %copy-start.9 = (s32[8]{0:T(128)S(1)}, s32[8]{0:T(128)}, u32[]{:S(2)}) copy-start(s32[8]{0:T(128)} %param.23) | copy-start | bytes 100
  232.2 1.9 copy-start.2
  235.0 116.5 %all-gather.8.cloned.1.call-start = ((), (), s32[]{:S(2)}) async-start(), calls=%async_computation.1 | async-start | bytes 2088960 | tf_op jit(solution)/shard_map/all_gather | solution.py:11
  235.6 212.1 %all-reduce.3.cloned.1.call-start = ((), (), s32[]{:S(2)}) async-start(), calls=%async_computation.2 | async-start | bytes 786432 | tf_op jit(solution)/shard_map/psum | solution.py:113
  488.7 20.7 %copy-start.1 = (bf16[10,8,32,384]{3,2,1,0:T(8,128)(2,1)S(1)}, bf16[10,8,32,384]{3,2,1,0:T(8,128)(2,1)}, u32[]{:S(2)}) copy-start(bf16[10,8,32,384]{3,2,1,0:T(8,128)(2,1)} %param.18) | copy-start | bytes 5898244
Sparse Core Ops, SparseCore 0:
  42.7 77.3 reduce-scatter.1
  123.2 48.5 all-gather.11
  174.3 46.8 all-gather.13
  235.1 67.3 all-gather.9
  304.8 46.7 all-gather.7
  381.2 66.4 all-reduce.2
where the time goes:
time: 523 us; the launch traced here: 516 us
  waiting for transfers between devices  223 us (43%)
  blocking collectives  97.4 us (19%)
  matrix products  75.1 us (14%)
  other arithmetic  66 us (13%)
  local copies, waits for them, and re-layouts  37.2 us (7%)
  between operations  15.9 us (3%)
    all_gather x4, waiting for transfers between devices, entering(): gathered = jax.tree.map(lambda a: lax.all_gather(a, axis), part)  103 us
    psum x1, waiting for transfers between devices, shards(): level_total = lax.psum(partial_value, 'mem')  61.3 us
    reduce_scatter x1, waiting for transfers between devices, shards(): lax.psum_scatter(spread, 'tile', scatter_dimension=0, tiled=True)  58.2 us
    unnamed x1, blocking collectives  40 us
    all_gather x1, blocking collectives, shards(): every_tile = lax.all_gather(low_blocks, 'tile', axis=0, tiled=True)  33.9 us
    add x30, other arithmetic, combine_steps(): late_rate[None, :, None] * leading_sum + late_sum  29.8 us
    dot_general x2, matrix products, filter_columns(): jnp.einsum('slyj,lij->slyi', values, column_filter, precision=lax.Precisi...  24.5 us
    all_gather x1, blocking collectives, shards(): all_levels = lax.all_gather(back_field, 'mem', axis=0, tiled=True)  23.5 us
  transfers between devices with their start and end apart: 6, of which 5 were waited for; matrix products, arithmetic and copies ran while one was open for 13% of the time, Pallas kernels for 0%

commit v1 on v0

v1 whole, which is shorter than its diff:
```python
import jax
import jax.numpy as jnp
from jax import lax
from jax.experimental import pallas as pl
from jax.experimental.pallas import tpu as pltpu
from jax.sharding import PartitionSpec as P

MESH = pl.DeviceIdType.MESH
F32 = jnp.float32
BF16 = jnp.bfloat16

LEVELS = 8
TILES = 16
ROWS = 32
COLS = 384
HALF = 5
PACK = HALF * ROWS
SLOTS = 128
BLK = 32
QROWS = ROWS * COLS // 128
DROWS = 384
GROUP = 4


def dot(a, b):
    return lax.dot_general(a, b, (((1,), (0,)), ((), ())), preferred_element_type=F32)


def dot_nt(a, b):
    return lax.dot_general(a, b, (((1,), (1,)), ((), ())), preferred_element_type=F32)


def split(x):
    high = x.astype(BF16)
    return high, (x - high.astype(F32)).astype(BF16)


def coefficient(a):
    t = 1.0 - a * a
    ratio = (t * t * t) / (1.0 + a * a)
    return jnp.where(ratio > 0.0, jnp.sqrt(jnp.sqrt(jnp.maximum(ratio, 1e-37))), 0.0)


def scans(a, pos, width, segment):
    logs = jnp.log(a)
    steps = [1 << b for b in range(16) if (1 << b) < segment]
    for k in steps:
        logs = logs + jnp.where(pos >= k, pltpu.roll(logs, k, 1), 0.0)
    rate = jnp.where(pos < segment - 1, pltpu.roll(a * a, width - 1, 1), 0.0)
    h = jnp.ones_like(a)
    for k in steps:
        h = h + rate * pltpu.roll(h, width - k, 1)
        rate = rate * pltpu.roll(rate, width - k, 1)
    return logs, h


def smooth(fields, carries, mt, pb, qb, kk, precise):
    p3 = jnp.concatenate([pb] * 3, axis=1)
    q3 = jnp.concatenate([qb] * 3, axis=1)
    rows = []
    for field, carry in zip(fields, carries):
        hi, *lo = field
        stack = jnp.concatenate([hi, hi, *lo], axis=0)
        y = dot(mt[:, 0 : stack.shape[0]], stack)
        for m in range(HALF):
            rows.append(
                y[ROWS * m : ROWS * m + ROWS]
                + p3 * carry[m : m + 1, :]
                + q3 * carry[8 + m : 9 + m, :]
            )
    y = jnp.concatenate(rows, axis=0)
    if not precise:
        yh = y.astype(BF16)
        return dot(jnp.concatenate([yh, yh], axis=1), kk)
    yh, yl = split(y)
    return dot(jnp.concatenate([yh, yh, yl], axis=1), jnp.concatenate([kk, kk[0:COLS]], axis=0))


def members(gm_ref):
    own = gm_ref[lax.axis_index("mem")]
    total = gm_ref[0]
    for i in range(1, LEVELS):
        total = total + gm_ref[i]
    scale = 1.0 / jnp.sqrt(jnp.full((1, COLS), total.astype(F32) - 1.0, F32))
    return scale, [jnp.where(m < own, 1.0, 0.0).astype(F32) for m in range(2 * HALF)]


def grad_kernel(
    gm_ref, pert_ref, back_ref, de_ref, mt_ref, pb_ref, qb_ref, kk_ref, inc_ref,
    inc_out, grad_ref,
):
    scale, live = members(gm_ref)
    fields = []
    for half in range(2):
        x = pert_ref[HALF * half : HALF * half + HALF, 0].astype(F32) * back_ref[...]
        fields.append(split(x.reshape(PACK, COLS)))
    y = smooth(
        fields, (de_ref[0], de_ref[1]), mt_ref[0], pb_ref[0], qb_ref[0], kk_ref[0], False
    )
    for m in range(2 * HALF):
        grad_ref[m, 0] = y[ROWS * m : ROWS * m + ROWS] * (scale * live[m])

    rows = DROWS // LEVELS
    first = pl.program_id(0) * rows
    x = inc_ref[pl.ds(pl.multiple_of(first, rows), rows), :]
    for r in range(rows):
        at = pl.multiple_of((first + r) * 128, 128)
        inc_out[0:1, pl.ds(at, 128)] = x[r : r + 1, :]


def kernel(
    alpha_hbm, pert_hbm, cot_hbm, dy_ref, dx_ref, gm_ref, w_hbm, pc_ref, src_hbm, dst_hbm,
    inc_hbm, back_hbm, de_hbm, mt_hbm, pb_hbm, qb_hbm, kk_hbm,
    alpha_v, pert_v, cot_raw, cot_v, w_v, src_v, dst_v,
    rep_v, yt, ytail, xt, mt, zf, zadd, pb, qb, kk,
    zs, zr, zo, de, zs2, zr2, zo2, de2,
    ss, sr, bq, back, ps, pr, lq, low, lows, inc_v, scol_v, dcol_v,
    in_sem, w_sem, out_sem, zs_s, zs_r, zo_s, zo_r, zs2_s, zs2_r, zo2_s, zo2_r,
    sp_s, sp_r, rs_s, rs_r, lo_s, lo_r, bk_s, bk_r,
):
    g = lax.axis_index("mem")
    t = lax.axis_index("tile")

    def tile_peer(k):
        return lax.rem(t + k, TILES)

    def tile_back(k):
        return lax.rem(t + TILES - k, TILES)

    def mem_peer(k):
        return lax.rem(g + k, LEVELS)

    def to_tile(src, dst, ssem, rsem, s):
        return pltpu.make_async_remote_copy(
            src_ref=src, dst_ref=dst, send_sem=ssem, recv_sem=rsem,
            device_id={"tile": s}, device_id_type=MESH,
        )

    def to_mem(src, dst, ssem, rsem, s):
        return pltpu.make_async_remote_copy(
            src_ref=src, dst_ref=dst, send_sem=ssem, recv_sem=rsem,
            device_id={"mem": s}, device_id_type=MESH,
        )

    loads = [
        pltpu.make_async_copy(alpha_hbm, alpha_v, in_sem.at[0]),
        pltpu.make_async_copy(cot_hbm, cot_raw, in_sem.at[1]),
        pltpu.make_async_copy(src_hbm.at[t], src_v, in_sem.at[2]),
        pltpu.make_async_copy(dst_hbm.at[t], dst_v, in_sem.at[3]),
        pltpu.make_async_copy(pert_hbm, pert_v, in_sem.at[4]),
    ]

    def wait_all(buf, sem, count):
        part = buf.at[pl.ds(0, count - 1)]
        pltpu.make_async_copy(part, part, sem).wait()

    def w_load(s):
        return pltpu.make_async_copy(w_hbm.at[0, s], w_v.at[s], w_sem.at[s])

    for c in loads[:4]:
        c.start()

    @pl.loop(1, TILES + 1)
    def _(k):
        w_load(tile_peer(k)).start()

    loads[4].start()

    barrier = pltpu.get_barrier_semaphore()

    @pl.loop(1, TILES)
    def _(k):
        pl.semaphore_signal(barrier, inc=1, device_id={"tile": tile_peer(k)}, device_id_type=MESH)

    @pl.loop(1, LEVELS)
    def _(k):
        pl.semaphore_signal(barrier, inc=1, device_id={"mem": mem_peer(k)}, device_id_type=MESH)

    scale, live = members(gm_ref)

    for k in range(16):
        rep_v[:, 32 * k : 32 * k + 32] = dy_ref[...]
    a = rep_v[...]
    pos = lax.broadcasted_iota(jnp.int32, (8, 512), 1) & 31
    logs, h = scans(a, pos, 512, ROWS)
    c = coefficient(a)
    ltot = jnp.broadcast_to(logs[:, 31:32], (8, 512))
    lane512 = lax.broadcasted_iota(jnp.int32, (8, 512), 1)
    hsum = jnp.sum(jnp.where(lane512 < 32, jnp.exp(2.0 * logs), 0.0), axis=1, keepdims=True)
    for f, x in enumerate(
        (logs, c, c * h, c * h * jnp.exp(logs), c * jnp.exp(ltot - logs))
    ):
        yt[:, f, :] = x
    yt[:, 5:8, :] = jnp.zeros((LEVELS, 3, 512), F32)
    ytail[:, 0, :] = jnp.broadcast_to(jnp.exp(ltot[:, 0:1]), (LEVELS, COLS))
    ytail[:, 1, :] = jnp.broadcast_to(hsum, (LEVELS, COLS))
    lane_y = lax.broadcasted_iota(jnp.int32, (ROWS, 512), 1)
    lower = lax.broadcasted_iota(jnp.int32, (ROWS, 512), 0) >= (lane_y & 31)
    zr_i = lax.broadcasted_iota(jnp.int32, (16, 256), 0)
    zc_i = lax.broadcasted_iota(jnp.int32, (16, 256), 1) >> 5
    row16 = lax.broadcasted_iota(jnp.int32, (16, COLS), 0)

    def columns(rows):
        width = rows.shape[1]
        return jnp.transpose(jnp.concatenate([rows, jnp.zeros((120, width), F32)], axis=0))

    @pl.loop(0, LEVELS)
    def _(l):
        rows = yt[l]
        cols = columns(rows[:, 0:128])[0:ROWS]

        def col(f):
            return cols[:, f : f + 1]

        e = jnp.exp(-jnp.abs(col(0) - rows[0:1]))
        m = e * jnp.where(lower, col(2) * rows[1:2], col(1) * rows[2:3])
        part = lane_y >> 5
        mh, ml = split(m)
        m = jnp.where((part >= HALF) & (part < 2 * HALF), ml.astype(F32), mh.astype(F32))
        part = jnp.where(part < 3 * HALF, part % HALF, -1)
        for i in range(HALF):
            mt[l, ROWS * i : ROWS * i + ROWS, :] = jnp.where(part == i, m, 0.0).astype(BF16)
        z = jnp.where(zr_i == zc_i, rows[4:5, 0:256], 0.0) + jnp.where(zr_i == zc_i + 8, rows[3:4, 0:256], 0.0)
        z = jnp.where(zc_i < HALF, z, 0.0)
        zh, zl = split(z)
        zf[l, 0:16, :] = zh[:, 0:PACK]
        zf[l, 16:32, :] = zl[:, 0:PACK]
        tail = ytail[l]
        zadd[l] = jnp.where(row16 == 5, tail[0:1], 0.0) + jnp.where(row16 == 6, tail[1:2], 0.0)
        pb[l] = jnp.broadcast_to(col(3), (ROWS, 128))
        qb[l] = jnp.broadcast_to(col(4), (ROWS, 128))

    low[:, QROWS:128, :] = jnp.zeros((TILES, 128 - QROWS, 128), BF16)

    loads[1].wait()

    @pl.loop(0, DROWS // 16)
    def _(i):
        rows = [
            cot_raw[:, pl.ds(pl.multiple_of(2048 * i + 128 * r, 128), 128)].astype(F32)
            for r in range(16)
        ]
        cot_v[pl.ds(pl.multiple_of(16 * i, 16), 16), :] = jnp.concatenate(rows, axis=0).astype(BF16)

    loads[0].wait()
    pl.semaphore_wait(barrier, TILES - 1 + LEVELS - 1)

    def alpha_of(l, half):
        return alpha_v[HALF * half : HALF * half + HALF, l].reshape(PACK, COLS)

    def source(l, hi, lo=None):
        r = dot(zf[l], hi)
        z = r[0:16] + r[16:32] + zadd[l]
        if lo is not None:
            z = z + dot(zf[l, 0:16, :], lo)
        return z

    def sources(field, zs, zr, s_s, s_r, first, last):
        @pl.loop(first, last)
        def _(k):
            found = []
            for i in range(2):
                l = lax.rem(t // 2 + 2 * k + i + 1, LEVELS)
                for half in range(2):
                    found.append((2 * l + half, source(l, *field(l, half))))
            for tt, z in found:
                zs[tt] = z
            for tt, _z in found:

                @pl.when(tt != t)
                def _():
                    to_tile(zs.at[tt], zr.at[t], s_s, s_r, tt).start()

        if last == LEVELS // 2:
            zr[t] = zs[t]

    sources(lambda l, half: (alpha_of(l, half),), zs, zr, zs_s, zs_r, 0, LEVELS // 2)

    def recursion(zr, zo, de, s_r, o_s, o_r):
        wait_all(zr, s_r, TILES)
        d = jnp.zeros((8, COLS), F32)
        downs = []
        for s in range(TILES):
            downs.append(d)
            zo[s, 0:8, :] = d
            d = zr[s, 5:6, :] * d + zr[s, 0:8, :]
        e = jnp.zeros((8, COLS), F32)
        for s in reversed(range(TILES)):
            zo[s, 8:16, :] = e
            e = zr[s, 5:6, :] * e + (zr[s, 8:16, :] + zr[s, 6:7, :] * downs[s])

        @pl.loop(1, TILES)
        def _(k):
            s = tile_peer(k)
            to_tile(zo.at[s], de.at[t], o_s, o_r, s).start()

        de[t] = zo[t]

    lane1 = lax.broadcasted_iota(jnp.int32, (1, 128), 1)
    lane = lax.broadcasted_iota(jnp.int32, (SLOTS, 128), 1)
    lgroup = lane >> 5
    slot_id = lax.broadcasted_iota(jnp.int32, (SLOTS, 128), 0)
    r16 = lax.broadcasted_iota(jnp.int32, (16, 128), 0) - (
        lax.broadcasted_iota(jnp.int32, (16, 128), 1) >> 5
    )
    sub96 = lax.broadcasted_iota(jnp.int32, (QROWS, 128), 0)
    sub384 = lax.broadcasted_iota(jnp.int32, (DROWS, 128), 0)

    def one_hot(condition):
        return jnp.where(condition, 1.0, 0.0).astype(BF16)

    def source_row(s):
        return jnp.where(lane1 < pc_ref[t, s], src_v[pl.ds(s, 1), :], -1)

    def target_row(s):
        return dst_v[pl.ds(s, 1), :]

    def spread_out(x):
        x = x + pltpu.roll(x, 64, 1)
        return x + pltpu.roll(x, 32, 1)

    def back_terms(tiles):
        srows = [source_row(s) for s in tiles]
        scols = [scol_v[s] for s in tiles]
        dcols = [dcol_v[s] for s in tiles]
        pick = jnp.concatenate(
            [
                jnp.concatenate([one_hot(lane + 128 * k == dcol) for k in range(3)], axis=1)
                for dcol in dcols
            ],
            axis=0,
        )
        grad = dot(pick, cot_v[...]).astype(BF16)
        results = []
        for n, s in enumerate(tiles):
            parts = []
            for i in range(8):
                w = w_v[s, 16 * i : 16 * i + 16].reshape(16 * BLK, 128)
                o = dot_nt(grad[SLOTS * n + 16 * i : SLOTS * n + 16 * i + 16], w)
                parts.append(
                    sum(
                        jnp.where(r16 == 4 * j, o[:, 128 * j : 128 * j + 128], 0.0)
                        for j in range(4)
                    )
                )
            terms = spread_out(jnp.concatenate(parts, axis=0))
            terms = jnp.where(lgroup == (scols[n] & 3), terms, 0.0)
            put = one_hot(sub96 == (srows[n] >> 2))
            both = dot(put, jnp.concatenate(split(terms), axis=1))
            results.append((both[:, 0:128] + both[:, 128:256]).astype(BF16))
        return results

    def forward_terms(tiles):
        puts, sums = [], []
        for s in tiles:
            scol = scol_v[s]
            picked = dot(one_hot(lane == (scol >> 2)), low[s])
            picked = spread_out(jnp.where(lgroup == (scol & 3), picked, 0.0))
            parts = []
            for i in range(8):
                x = picked[16 * i : 16 * i + 16]
                x = jnp.concatenate([jnp.where(r16 == 4 * j, x, 0.0) for j in range(4)], axis=1)
                w = w_v[s, 16 * i : 16 * i + 16].reshape(16 * BLK, 128)
                parts.append(dot(x.astype(BF16), w))
            sums.append(jnp.concatenate(split(jnp.concatenate(parts, axis=0)), axis=1))
            puts.append(one_hot(sub384 == target_row(s)))
        both = dot(jnp.concatenate(puts, axis=1), jnp.concatenate(sums, axis=0))
        return both[:, 0:128] + both[:, 128:256]

    loads[2].wait()
    loads[3].wait()
    turned = jnp.transpose(
        jnp.concatenate([src_v[...], dst_v[...], jnp.zeros((96, SLOTS), jnp.int32)], axis=0).astype(F32)
    ).astype(jnp.int32)
    for s in range(TILES):
        scol = jnp.broadcast_to(turned[:, s : s + 1], (SLOTS, 128))
        scol_v[s] = jnp.where(slot_id < pc_ref[t, s], scol, -1)
        dcol_v[s] = jnp.broadcast_to(turned[:, TILES + s : TILES + s + 1], (SLOTS, 128))

    def back_step(j):
        tiles = [tile_peer(GROUP * j + 1 + i) for i in range(GROUP)]
        for s in tiles:
            w_load(s).wait()
        results = back_terms(tiles)
        for s, r in zip(tiles, results):
            ss[s] = r
        for s in tiles:

            @pl.when(s != t)
            def _():
                to_tile(ss.at[s], sr.at[t], sp_s, sp_r, s).start()

    steps = TILES // GROUP

    @pl.loop(0, steps)
    def _(j):
        back_step(j)

        @pl.when(j == steps // 2 - 1)
        def _():
            recursion(zr, zo, de, zs_r, zo_s, zo_r)

    sr[t] = ss[t]

    ax = dx_ref[...]
    posx = lax.broadcasted_iota(jnp.int32, (8, COLS), 1)
    lx, hx = scans(ax, posx, COLS, COLS)
    cx = coefficient(ax)
    gx = cx * hx
    edge1 = jnp.broadcast_to(lx[:, 127:128], (8, COLS))
    edge2 = jnp.broadcast_to(lx[:, 255:256], (8, COLS))
    xt[:, 0, :] = lx
    xt[:, 1, :] = cx
    xt[:, 2, :] = gx
    xt[:, 3, :] = gx * jnp.exp(jnp.minimum(lx - jnp.where(posx < 256, edge1, edge2), 0.0))
    xt[:, 4, :] = cx * jnp.exp(jnp.minimum(edge1 - lx, 0.0))
    xt[:, 5, :] = cx * jnp.exp(jnp.minimum(edge2 - lx, 0.0))
    xt[:, 6:8, :] = jnp.zeros((LEVELS, 2, COLS), F32)
    lowx = lax.broadcasted_iota(jnp.int32, (128, 128), 0) >= (
        lax.broadcasted_iota(jnp.int32, (128, 128), 1)
    )

    @pl.loop(0, LEVELS)
    def _(l):
        rows = xt[l]
        cols = columns(rows)
        for ib in range(3):
            for jb in range(3):
                r = rows[:, 128 * jb : 128 * jb + 128]

                def xcol(f):
                    return cols[128 * ib : 128 * ib + 128, f : f + 1]

                if ib == jb:
                    e = jnp.exp(-jnp.abs(xcol(0) - r[0:1]))
                    m = e * jnp.where(lowx, xcol(2) * r[1:2], xcol(1) * r[2:3])
                elif ib > jb:
                    m = xcol(3) * r[3 + ib : 4 + ib]
                else:
                    m = xcol(3 + jb) * r[3:4]
                mh, ml = split(m)
                kk[l, 128 * ib : 128 * ib + 128, 128 * jb : 128 * jb + 128] = mh
                at = COLS + 128 * ib
                kk[l, at : at + 128, 128 * jb : 128 * jb + 128] = ml

    exports = [
        pltpu.make_async_copy(x, y, out_sem.at[i])
        for i, (x, y) in enumerate(
            [
                (mt, mt_hbm), (pb, pb_hbm), (qb, qb_hbm), (kk, kk_hbm),
                (back, back_hbm), (de2, de_hbm), (inc_v, inc_hbm),
            ]
        )
    ]
    for x in exports[:4]:
        x.start()

    wait_all(sr, sp_r, TILES)
    acc = sr[0].astype(F32)
    for s in range(1, TILES):
        acc = acc + sr[s].astype(F32)
    bq[...] = acc
    for j in range(3):
        back[g, :, 128 * j : 128 * j + 128] = bq[pl.ds(j, ROWS, stride=3), :]

    @pl.loop(1, LEVELS)
    def _(k):
        l = mem_peer(k)
        to_mem(back.at[g], back.at[g], bk_s, bk_r, l).start()

    loads[4].wait()
    wait_all(de, zo_r, TILES)

    def partial(l):
        y = smooth(
            [(alpha_of(l, half),) for half in range(2)], (de[2 * l], de[2 * l + 1]),
            mt[l], pb[l], qb[l], kk[l], True,
        )
        acc = jnp.zeros((ROWS, COLS), F32)
        for m in range(2 * HALF):
            acc = acc + (live[m] * pert_v[m, l].astype(F32)) * y[ROWS * m : ROWS * m + ROWS]
        return acc

    @pl.loop(1, LEVELS + 1)
    def _(k):
        l = mem_peer(k)
        ps[l] = partial(l)

        @pl.when(l != g)
        def _():
            to_mem(ps.at[l], pr.at[g], rs_s, rs_r, l).start()

    pr[g] = ps[g]

    wait_all(back, bk_r, LEVELS)
    exports[4].start()

    def weighted(l, half):
        x = pert_v[HALF * half : HALF * half + HALF, l].astype(F32) * back[l][None]
        return split(x.reshape(PACK, COLS))

    sources(weighted, zs2, zr2, zs2_s, zs2_r, 0, 2)

    wait_all(pr, rs_r, LEVELS)
    acc = pr[0]
    for s in range(1, LEVELS):
        acc = acc + pr[s]
    acc = acc * scale
    for j in range(3):
        lq[pl.ds(j, ROWS, stride=3), :] = acc[:, 128 * j : 128 * j + 128]
    lows[...] = lq[...].astype(BF16)

    @pl.loop(1, TILES)
    def _(k):
        s = tile_peer(k)
        to_tile(lows, low.at[t, pl.ds(0, QROWS), :], lo_s, lo_r.at[t], s).start()

    low[t, 0:QROWS, :] = lows[...]

    sources(weighted, zs2, zr2, zs2_s, zs2_r, 2, 4)

    inc_v[...] = jnp.zeros((DROWS, 128), F32)

    def forward_step(j):
        for i in range(GROUP):
            s = tile_back(GROUP * j + i)

            @pl.when(s != t)
            def _():
                to_tile(lows, low.at[s, pl.ds(0, QROWS), :], lo_s, lo_r.at[s], s).wait_recv()

        inc_v[...] += forward_terms([tile_back(GROUP * j + i) for i in range(GROUP)])

    @pl.loop(0, steps)
    def _(j):
        forward_step(j)

        @pl.when(j == steps // 2 - 1)
        def _():
            recursion(zr2, zo2, de2, zs2_r, zo2_s, zo2_r)

    wait_all(de2, zo2_r, TILES)
    exports[5].start()
    exports[6].start()

    wait_all(zs, zs_s, TILES)
    wait_all(zo, zo_s, TILES)
    wait_all(zs2, zs2_s, TILES)
    wait_all(zo2, zo2_s, TILES)
    wait_all(ss, sp_s, TILES)
    wait_all(sr, lo_s, TILES)
    wait_all(ps, rs_s, LEVELS)
    wait_all(back, bk_s, LEVELS)
    for x in exports:
        x.wait()


def shards(
    alpha, perturbation, cotangent, decay_y, decay_x, group_members, interp_weight,
    pair_count, src_index, dst_index,
):
    any_spec = pl.BlockSpec(memory_space=pl.ANY)
    vmem = pl.BlockSpec(memory_space=pltpu.VMEM)
    smem = pl.BlockSpec(memory_space=pltpu.SMEM)
    dma = pltpu.SemaphoreType.DMA
    V = pltpu.VMEM
    zbuf = V((TILES, 16, COLS), F32)
    scratch = [
        V((2 * HALF, LEVELS, ROWS, COLS), BF16),
        V((2 * HALF, LEVELS, ROWS, COLS), BF16),
        V((1, DROWS * 128), BF16),
        V((DROWS, 128), BF16),
        V((TILES, SLOTS, BLK, 128), BF16),
        V((TILES, SLOTS), jnp.int32),
        V((TILES, SLOTS), jnp.int32),
        V((8, 512), F32),
        V((LEVELS, 8, 512), F32),
        V((LEVELS, 2, COLS), F32),
        V((LEVELS, 8, COLS), F32),
        V((LEVELS, PACK, 512), BF16),
        V((LEVELS, 32, PACK), BF16),
        V((LEVELS, 16, COLS), F32),
        V((LEVELS, ROWS, 128), F32),
        V((LEVELS, ROWS, 128), F32),
        V((LEVELS, 2 * COLS, COLS), BF16),
        *[zbuf] * 8,
        V((TILES, QROWS, 128), BF16),
        V((TILES, QROWS, 128), BF16),
        V((QROWS, 128), F32),
        V((LEVELS, ROWS, COLS), F32),
        V((LEVELS, ROWS, COLS), F32),
        V((LEVELS, ROWS, COLS), F32),
        V((QROWS, 128), F32),
        V((TILES, 128, 128), BF16),
        V((QROWS, 128), BF16),
        V((DROWS, 128), F32),
        V((TILES, SLOTS, 128), jnp.int32),
        V((TILES, SLOTS, 128), jnp.int32),
        dma((5,)),
        dma((TILES,)),
        dma((7,)),
        *[dma] * 12,
        dma,
        dma((TILES,)),
        dma,
        dma,
    ]
    shape = jax.ShapeDtypeStruct
    inc, *rest = pl.pallas_call(
        kernel,
        out_shape=(
            shape((DROWS, 128), F32),
            shape((LEVELS, ROWS, COLS), F32),
            shape((TILES, 16, COLS), F32),
            shape((LEVELS, PACK, 512), BF16),
            shape((LEVELS, ROWS, 128), F32),
            shape((LEVELS, ROWS, 128), F32),
            shape((LEVELS, 2 * COLS, COLS), BF16),
        ),
        in_specs=[any_spec, any_spec, any_spec, vmem, vmem, smem, any_spec, smem, any_spec, any_spec],
        out_specs=(any_spec,) * 7,
        scratch_shapes=scratch,
        compiler_params=pltpu.CompilerParams(
            collective_id=0, has_side_effects=True, vmem_limit_bytes=60 * 1024 * 1024
        ),
        cost_estimate=pl.CostEstimate(
            flops=9_000_000_000, bytes_accessed=29_000_000, transcendentals=700_000
        ),
    )(
        alpha, perturbation, cotangent, decay_y, decay_x, group_members,
        interp_weight, pair_count, src_index, dst_index,
    )

    def level(*block):
        return pl.BlockSpec(block, lambda l: (l,) + (0,) * (len(block) - 1))

    member_block = pl.BlockSpec((2 * HALF, 1, ROWS, COLS), lambda l: (0, l, 0, 0))
    return pl.pallas_call(
        grad_kernel,
        grid=(LEVELS,),
        out_shape=(shape((1, DROWS * 128), F32), shape(alpha.shape, F32)),
        in_specs=[
            smem,
            member_block,
            level(1, ROWS, COLS),
            level(2, 16, COLS),
            level(1, PACK, 512),
            level(1, ROWS, 128),
            level(1, ROWS, 128),
            level(1, 2 * COLS, COLS),
            pl.BlockSpec((DROWS, 128), lambda l: (0, 0)),
        ],
        out_specs=(pl.BlockSpec((1, DROWS * 128), lambda l: (0, 0)), member_block),
        compiler_params=pltpu.CompilerParams(vmem_limit_bytes=60 * 1024 * 1024),
        cost_estimate=pl.CostEstimate(
            flops=3_500_000_000, bytes_accessed=13_000_000, transcendentals=0
        ),
    )(group_members, perturbation, *rest, inc)


def solution(mesh):
    in_specs = (
        P("mem", None, "tile", None),
        P("mem", None, "tile", None),
        P("mem", "tile"),
        P(None, "tile"),
        P(),
        P(),
        P("tile", None, None, None, None),
        P(),
        P(),
        P(),
    )
    out_specs = (P("mem", "tile"), P("mem", None, "tile", None))
    return jax.shard_map(shards, mesh=mesh, in_specs=in_specs, out_specs=out_specs, check_vma=False)
```

time: 523 us -> 70 us (0.13); the launches traced: 516 us -> 69.6 us
  waiting for transfers between devices: 223 us -> 0 us
  blocking collectives: 97.4 us -> 0 us
  matrix products: 75.1 us -> 0 us
  Pallas kernels: 0 us -> 69 us
  other arithmetic: 66 us -> 0 us
  local copies, waits for them, and re-layouts: 37.2 us -> 0 us
  between operations: 15.9 us -> 0.64 us
    all_gather x4 -> x0, waiting for transfers between devices: 103 us -> none  [entering(): gathered = jax.tree.map(lambda a: lax.all_gather(a, axis), part)]
    dot_general x9 -> x0, matrix products: 75.1 us -> none  [the longest x2 24.5 us: filter_columns(): jnp.einsum('slyj,lij->slyi', values, column_filter, precision=lax.Precisi...]
    pallas_call x0 -> x2, Pallas kernels: none -> 69 us  [the longest x1 58.8 us: shards(): pl.pallas_call(kernel, out_shape=(shape((DROWS, 128), F32), shape((LEVELS...]
    psum x1 -> x0, waiting for transfers between devices: 61.3 us -> none  [shards(): level_total = lax.psum(partial_value, 'mem')]
    reduce_scatter x1 -> x0, waiting for transfers between devices: 58.2 us -> none  [shards(): lax.psum_scatter(spread, 'tile', scatter_dimension=0, tiled=True)]
    all_gather x2 -> x0, blocking collectives: 57.4 us -> none  [the longest x1 33.9 us: shards(): every_tile = lax.all_gather(low_blocks, 'tile', axis=0, tiled=True)]
    unnamed x1 -> x0, blocking collectives: 40 us -> none
    add x31 -> x0, other arithmetic: 29.8 us -> none  [the longest x30 29.8 us: combine_steps(): late_rate[None, :, None] * leading_sum + late_sum]
  transfers between devices with their start and end apart: 6 -> 0, of which waited for: 5 -> 0; matrix products, arithmetic and copies ran while one was open for 13% -> 0% of each run, Pallas kernels for 0% -> 0%
where the time goes in v1:
time: 70 us; the launch traced here: 69.6 us
  Pallas kernels  69 us (99%)
    pallas_call x1, Pallas kernels, shards(): pl.pallas_call(kernel, out_shape=(shape((DROWS, 128), F32), shape((LEVELS...  58.8 us
    pallas_call x1, Pallas kernels, shards(): pl.pallas_call(grad_kernel, grid=(LEVELS,), out_shape=(shape((1, DROWS *...  10.2 us

profile of v1, /device:TPU:1, one launch (start us, length us, event | category | flops | bytes accessed | tf_op | source)
XLA Modules:
  0.0 69.6 jit_solution(5959219285537557979)
XLA Ops:
  0.6 58.8 %shard_map.113 = (f32[384,128]{1,0:T(8,128)}, f32[8,32,384]{2,1,0:T(8,128)}, f32[16,16,384]{2,1,0:T(8,128)}, bf16[8,160,512]{2,1,0:T(8,128)(2,1)}, f32[8,32,128]...) custom-call(bf16[10,8,32,384]{3,2,1,0:T(8,128)(2,1)} %alpha_hbm.1, ...), custom_call_target="tpu_custom_call" | custom-call | flops 8999999488 | bytes 29000000 | tf_op jit(solution)/shard_map/pallas_call | solution.py:609
  59.5 10.2 %shard_map.114 = (f32[1,49152]{1,0:T(1,128)}, f32[10,8,32,384]{3,2,1,0:T(8,128)}) custom-call(s32[8]{0:T(128)} %gm_ref.3, bf16[10,8,32,384]{3,2,1,0:T(8,128)(2,1)} %pert_ref.1, f32[8,32,384]{2,1,0:T(8,128)} %get-tuple-element.9.back_ref, f32[16,16,384]{2,1,0:T(8,128)} %get-tuple-element.10.de_ref, bf16[8,160,512]{2,1,0:T(8,128)(2,1)} %get-tuple-element.11.mt_ref, ...), custom_call_target="tpu_custom_call" | custom-call | flops 3500000000 | bytes 13000000 | tf_op jit(solution)/shard_map/pallas_call | solution.py:638

commit v2 on v1

--- a/solution.py
+++ b/solution.py
@@ -319,6 +319,15 @@
         x = x + pltpu.roll(x, 64, 1)
         return x + pltpu.roll(x, 32, 1)
 
+    def weight_pair(s, i):
+        return jnp.concatenate(
+            [
+                w_v[s, 16 * (i + half) : 16 * (i + half) + 16].reshape(16 * BLK, 128)
+                for half in range(2)
+            ],
+            axis=1,
+        )
+
     def back_terms(tiles):
         srows = [source_row(s) for s in tiles]
         scols = [scol_v[s] for s in tiles]
@@ -334,15 +343,28 @@
         results = []
         for n, s in enumerate(tiles):
             parts = []
-            for i in range(8):
-                w = w_v[s, 16 * i : 16 * i + 16].reshape(16 * BLK, 128)
-                o = dot_nt(grad[SLOTS * n + 16 * i : SLOTS * n + 16 * i + 16], w)
-                parts.append(
-                    sum(
-                        jnp.where(r16 == 4 * j, o[:, 128 * j : 128 * j + 128], 0.0)
-                        for j in range(4)
+            for i in range(0, 8, 2):
+                first = SLOTS * n + 16 * i
+                zero = jnp.zeros((16, 128), BF16)
+                pair = jnp.concatenate(
+                    [
+                        jnp.concatenate([grad[first : first + 16], zero], axis=1),
+                        jnp.concatenate([zero, grad[first + 16 : first + 32]], axis=1),
+                    ],
+                    axis=0,
+                )
+                o = dot_nt(pair, weight_pair(s, i))
+                for half in range(2):
+                    parts.append(
+                        sum(
+                            jnp.where(
+                                r16 == 4 * j,
+                                o[16 * half : 16 * half + 16, 128 * j : 128 * j + 128],
+                                0.0,
+                            )
+                            for j in range(4)
+                        )
                     )
-                )
             terms = spread_out(jnp.concatenate(parts, axis=0))
             terms = jnp.where(lgroup == (scols[n] & 3), terms, 0.0)
             put = one_hot(sub96 == (srows[n] >> 2))
@@ -357,11 +379,16 @@
             picked = dot(one_hot(lane == (scol >> 2)), low[s])
             picked = spread_out(jnp.where(lgroup == (scol & 3), picked, 0.0))
             parts = []
-            for i in range(8):
-                x = picked[16 * i : 16 * i + 16]
-                x = jnp.concatenate([jnp.where(r16 == 4 * j, x, 0.0) for j in range(4)], axis=1)
-                w = w_v[s, 16 * i : 16 * i + 16].reshape(16 * BLK, 128)
-                parts.append(dot(x.astype(BF16), w))
+            for i in range(0, 8, 2):
+                xs = []
+                for half in range(2):
+                    x = picked[16 * (i + half) : 16 * (i + half) + 16]
+                    xs.append(
+                        jnp.concatenate([jnp.where(r16 == 4 * j, x, 0.0) for j in range(4)], axis=1)
+                    )
+                both = dot(jnp.concatenate(xs, axis=0).astype(BF16), weight_pair(s, i))
+                parts.append(both[0:16, 0:128])
+                parts.append(both[16:32, 128:256])
             sums.append(jnp.concatenate(split(jnp.concatenate(parts, axis=0)), axis=1))
             puts.append(one_hot(sub384 == target_row(s)))
         both = dot(jnp.concatenate(puts, axis=1), jnp.concatenate(sums, axis=0))

time: 70 us -> 70.1 us (level)
  no operation moved by 1% of the time
where the time goes in v2:
time: 70.1 us; the launch traced here: 69.7 us
  Pallas kernels  69 us (98%)
    pallas_call x1, Pallas kernels, shards(): pl.pallas_call(kernel, out_shape=(shape((DROWS, 128), F32), shape((LEVELS...  58.9 us
    pallas_call x1, Pallas kernels, shards(): pl.pallas_call(grad_kernel, grid=(LEVELS,), out_shape=(shape((1, DROWS *...  10.2 us

profile of v2, /device:TPU:1, one launch (start us, length us, event | category | flops | bytes accessed | tf_op | source)
XLA Modules:
  0.0 69.7 jit_solution(17278620967802102988)
XLA Ops:
  0.6 58.9 %shard_map.113 = (f32[384,128]{1,0:T(8,128)}, f32[8,32,384]{2,1,0:T(8,128)}, f32[16,16,384]{2,1,0:T(8,128)}, bf16[8,160,512]{2,1,0:T(8,128)(2,1)}, f32[8,32,128]...) custom-call(bf16[10,8,32,384]{3,2,1,0:T(8,128)(2,1)} %alpha_hbm.1, ...), custom_call_target="tpu_custom_call" | custom-call | flops 8999999488 | bytes 29000000 | tf_op jit(solution)/shard_map/pallas_call | solution.py:636
  59.5 10.2 %shard_map.114 = (f32[1,49152]{1,0:T(1,128)}, f32[10,8,32,384]{3,2,1,0:T(8,128)}) custom-call(s32[8]{0:T(128)} %gm_ref.3, bf16[10,8,32,384]{3,2,1,0:T(8,128)(2,1)} %pert_ref.1, f32[8,32,384]{2,1,0:T(8,128)} %get-tuple-element.9.back_ref, f32[16,16,384]{2,1,0:T(8,128)} %get-tuple-element.10.de_ref, bf16[8,160,512]{2,1,0:T(8,128)(2,1)} %get-tuple-element.11.mt_ref, ...), custom_call_target="tpu_custom_call" | custom-call | flops 3500000000 | bytes 13000000 | tf_op jit(solution)/shard_map/pallas_call | solution.py:665

commit v3 on v2

--- a/solution.py
+++ b/solution.py
@@ -11,6 +11,7 @@
 
 LEVELS = 8
 TILES = 16
+CHIPS = 8
 ROWS = 32
 COLS = 384
 HALF = 5
@@ -19,7 +20,7 @@
 BLK = 32
 QROWS = ROWS * COLS // 128
 DROWS = 384
-GROUP = 4
+GROUP = 2
 
 
 def dot(a, b):
@@ -54,7 +55,12 @@
     return logs, h
 
 
-def smooth(fields, carries, mt, pb, qb, kk, precise):
+def carry_row(carry, first):
+    rows = [carry[first + HALF * j : first + HALF * j + 1, :] for j in range(3)]
+    return jnp.concatenate(rows, axis=1)
+
+
+def smooth(fields, carries, mt, pb, qb, upper, lower=None):
     p3 = jnp.concatenate([pb] * 3, axis=1)
     q3 = jnp.concatenate([qb] * 3, axis=1)
     rows = []
@@ -65,15 +71,15 @@
         for m in range(HALF):
             rows.append(
                 y[ROWS * m : ROWS * m + ROWS]
-                + p3 * carry[m : m + 1, :]
-                + q3 * carry[8 + m : 9 + m, :]
+                + p3 * carry_row(carry, m)
+                + q3 * carry_row(carry, 16 + m)
             )
-    y = jnp.concatenate(rows, axis=0)
-    if not precise:
-        yh = y.astype(BF16)
-        return dot(jnp.concatenate([yh, yh], axis=1), kk)
-    yh, yl = split(y)
-    return dot(jnp.concatenate([yh, yh, yl], axis=1), jnp.concatenate([kk, kk[0:COLS]], axis=0))
+    yh, yl = split(jnp.concatenate(rows, axis=0))
+    if lower is None:
+        return dot(jnp.concatenate([yh, yl], axis=1), jnp.concatenate([upper] * 2, axis=0))
+    return dot(
+        jnp.concatenate([yh, yl, yh], axis=1), jnp.concatenate([upper, upper, lower], axis=0)
+    )
 
 
 def members(gm_ref):
@@ -86,46 +92,83 @@
 
 
 def grad_kernel(
-    gm_ref, pert_ref, back_ref, de_ref, mt_ref, pb_ref, qb_ref, kk_ref, inc_ref,
-    inc_out, grad_ref,
+    gm_ref, pert_hbm, back_hbm, de_hbm, mt_hbm, pb_hbm, qb_hbm, kk_hbm, inc_ref,
+    inc_out, grad_hbm,
+    pert_v, back_v, de_v, mt_v, pb_v, qb_v, kk_v, out_v, in_sem, out_sem,
 ):
+    def loads(l):
+        pairs = [
+            (pert_hbm.at[:, l], pert_v.at[:, l]),
+            (back_hbm.at[l], back_v.at[l]),
+            (de_hbm.at[:, l], de_v.at[:, l]),
+            (mt_hbm.at[l], mt_v.at[l]),
+            (pb_hbm.at[l], pb_v.at[l]),
+            (qb_hbm.at[l], qb_v.at[l]),
+            (kk_hbm.at[l], kk_v.at[l]),
+        ]
+        return [
+            pltpu.make_async_copy(a, b, in_sem.at[i, l]) for i, (a, b) in enumerate(pairs)
+        ]
+
+    def store(l):
+        return pltpu.make_async_copy(out_v.at[:, l], grad_hbm.at[:, l], out_sem.at[l])
+
+    @pl.loop(0, LEVELS)
+    def _(l):
+        for x in loads(l):
+            x.start()
+
     scale, live = members(gm_ref)
-    fields = []
-    for half in range(2):
-        x = pert_ref[HALF * half : HALF * half + HALF, 0].astype(F32) * back_ref[...]
-        fields.append(split(x.reshape(PACK, COLS)))
-    y = smooth(
-        fields, (de_ref[0], de_ref[1]), mt_ref[0], pb_ref[0], qb_ref[0], kk_ref[0], False
-    )
-    for m in range(2 * HALF):
-        grad_ref[m, 0] = y[ROWS * m : ROWS * m + ROWS] * (scale * live[m])
-
-    rows = DROWS // LEVELS
-    first = pl.program_id(0) * rows
-    x = inc_ref[pl.ds(pl.multiple_of(first, rows), rows), :]
-    for r in range(rows):
-        at = pl.multiple_of((first + r) * 128, 128)
-        inc_out[0:1, pl.ds(at, 128)] = x[r : r + 1, :]
+
+    @pl.loop(0, DROWS // 8)
+    def _(i):
+        x = inc_ref[pl.ds(pl.multiple_of(8 * i, 8), 8), :]
+        for r in range(8):
+            inc_out[0:1, pl.ds(pl.multiple_of(1024 * i + 128 * r, 128), 128)] = x[r : r + 1, :]
+
+    @pl.loop(0, LEVELS)
+    def _(l):
+        for x in loads(l):
+            x.wait()
+        fields = []
+        for half in range(2):
+            x = pert_v[HALF * half : HALF * half + HALF, l].astype(F32) * back_v[l][None]
+            fields.append(split(x.reshape(PACK, COLS)))
+        y = smooth(fields, (de_v[0, l], de_v[1, l]), mt_v[l], pb_v[l], qb_v[l], kk_v[l])
+        for m in range(2 * HALF):
+            out_v[m, l] = y[ROWS * m : ROWS * m + ROWS] * (scale * live[m])
+        store(l).start()
+
+    @pl.loop(0, LEVELS)
+    def _(l):
+        store(l).wait()
 
 
 def kernel(
     alpha_hbm, pert_hbm, cot_hbm, dy_ref, dx_ref, gm_ref, w_hbm, pc_ref, src_hbm, dst_hbm,
     inc_hbm, back_hbm, de_hbm, mt_hbm, pb_hbm, qb_hbm, kk_hbm,
     alpha_v, pert_v, cot_raw, cot_v, w_v, src_v, dst_v,
-    rep_v, yt, ytail, xt, mt, zf, zadd, pb, qb, kk,
-    zs, zr, zo, de, zs2, zr2, zo2, de2,
-    ss, sr, bq, back, ps, pr, lq, low, lows, inc_v, scol_v, dcol_v,
-    in_sem, w_sem, out_sem, zs_s, zs_r, zo_s, zo_r, zs2_s, zs2_r, zo2_s, zo2_r,
-    sp_s, sp_r, rs_s, rs_r, lo_s, lo_r, bk_s, bk_r,
+    rep_v, yt, ytail, xt, mt, zf, pb, qb, kk,
+    za, zp, zc, zr, zo, dc, dp, de, za2, zp2, zc2, zr2, zo2, dc2, dp2, de2,
+    sf, sp, ss, sr, bq, back, ps, pr, lq, low, lows, inc_v, scol_v, dcol_v,
+    in_sem, w_sem, out_sem, z_sem, z2_sem,
+    sp_s, sp_r, ss_s, ss_r, rs_s, rs_r, lo_s, lo_f, lo_r, bk_s, bk_r,
 ):
     g = lax.axis_index("mem")
     t = lax.axis_index("tile")
 
-    def tile_peer(k):
-        return lax.rem(t + k, TILES)
-
-    def tile_back(k):
-        return lax.rem(t + TILES - k, TILES)
+    chip = t // 2
+    core = lax.rem(t, 2)
+    partner = t + 1 - 2 * core
+
+    def chip_peer(k):
+        return lax.rem(chip + k, CHIPS)
+
+    def chip_back(k):
+        return lax.rem(chip + CHIPS - k, CHIPS)
+
+    def tile_of(ch):
+        return 2 * ch + core
 
     def mem_peer(k):
         return lax.rem(g + k, LEVELS)
@@ -157,20 +200,23 @@
     def w_load(s):
         return pltpu.make_async_copy(w_hbm.at[0, s], w_v.at[s], w_sem.at[s])
 
-    for c in loads[:4]:
+    for c in loads:
         c.start()
 
-    @pl.loop(1, TILES + 1)
+    @pl.loop(0, TILES)
+    def _(i):
+        late = i // CHIPS
+        w_load(2 * chip_peer(i - CHIPS * late + 1) + 1 - core + late * (2 * core - 1)).start()
+
+    barrier = pltpu.get_barrier_semaphore()
+
+    pl.semaphore_signal(barrier, inc=1, device_id={"tile": partner}, device_id_type=MESH)
+
+    @pl.loop(1, CHIPS)
     def _(k):
-        w_load(tile_peer(k)).start()
-
-    loads[4].start()
-
-    barrier = pltpu.get_barrier_semaphore()
-
-    @pl.loop(1, TILES)
-    def _(k):
-        pl.semaphore_signal(barrier, inc=1, device_id={"tile": tile_peer(k)}, device_id_type=MESH)
+        pl.semaphore_signal(
+            barrier, inc=1, device_id={"tile": tile_of(chip_peer(k))}, device_id_type=MESH
+        )
 
     @pl.loop(1, LEVELS)
     def _(k):
@@ -198,7 +244,6 @@
     lower = lax.broadcasted_iota(jnp.int32, (ROWS, 512), 0) >= (lane_y & 31)
     zr_i = lax.broadcasted_iota(jnp.int32, (16, 256), 0)
     zc_i = lax.broadcasted_iota(jnp.int32, (16, 256), 1) >> 5
-    row16 = lax.broadcasted_iota(jnp.int32, (16, COLS), 0)
 
     def columns(rows):
         width = rows.shape[1]
@@ -225,8 +270,6 @@
         zh, zl = split(z)
         zf[l, 0:16, :] = zh[:, 0:PACK]
         zf[l, 16:32, :] = zl[:, 0:PACK]
-        tail = ytail[l]
-        zadd[l] = jnp.where(row16 == 5, tail[0:1], 0.0) + jnp.where(row16 == 6, tail[1:2], 0.0)
         pb[l] = jnp.broadcast_to(col(3), (ROWS, 128))
         qb[l] = jnp.broadcast_to(col(4), (ROWS, 128))
 
@@ -243,58 +286,111 @@
         cot_v[pl.ds(pl.multiple_of(16 * i, 16), 16), :] = jnp.concatenate(rows, axis=0).astype(BF16)
 
     loads[0].wait()
-    pl.semaphore_wait(barrier, TILES - 1 + LEVELS - 1)
+    pl.semaphore_wait(barrier, 1 + CHIPS - 1 + LEVELS - 1)
 
     def alpha_of(l, half):
         return alpha_v[HALF * half : HALF * half + HALF, l].reshape(PACK, COLS)
 
     def source(l, hi, lo=None):
         r = dot(zf[l], hi)
-        z = r[0:16] + r[16:32] + zadd[l]
+        z = r[0:16] + r[16:32]
         if lo is not None:
             z = z + dot(zf[l, 0:16, :], lo)
         return z
 
-    def sources(field, zs, zr, s_s, s_r, first, last):
+    def sources(field, za, first, last):
         @pl.loop(first, last)
         def _(k):
             found = []
             for i in range(2):
-                l = lax.rem(t // 2 + 2 * k + i + 1, LEVELS)
+                l = 2 * k + i
                 for half in range(2):
-                    found.append((2 * l + half, source(l, *field(l, half))))
-            for tt, z in found:
-                zs[tt] = z
-            for tt, _z in found:
-
-                @pl.when(tt != t)
-                def _():
-                    to_tile(zs.at[tt], zr.at[t], s_s, s_r, tt).start()
-
-        if last == LEVELS // 2:
-            zr[t] = zs[t]
-
-    sources(lambda l, half: (alpha_of(l, half),), zs, zr, zs_s, zs_r, 0, LEVELS // 2)
-
-    def recursion(zr, zo, de, s_r, o_s, o_r):
-        wait_all(zr, s_r, TILES)
-        d = jnp.zeros((8, COLS), F32)
+                    found.append((half, l, source(l, *field(l, half))))
+            for half, l, z in found:
+                for j in range(3):
+                    part = z[:, 128 * j : 128 * j + 128]
+                    za[half, l, HALF * j : HALF * j + HALF, :] = part[0:HALF]
+                    za[half, l, 16 + HALF * j : 16 + HALF * j + HALF, :] = part[8 : 8 + HALF]
+                za[half, l, 15:16, :] = ytail[l, 0:1, 0:128]
+                za[half, l, 31:32, :] = ytail[l, 1:2, 0:128]
+
+    def to_partner(za, zp, sem):
+        other = za.at[1 - core]
+        return to_tile(other, zp, sem.at[0], sem.at[1], partner)
+
+    row16 = lax.broadcasted_iota(jnp.int32, (16, 128), 0)
+
+    def tile_maps(za, zp, l):
+        own, theirs = za[core, l], zp[l]
+        first = jnp.where(core == 0, own, theirs)
+        second = jnp.where(core == 0, theirs, own)
+        return [(x[0:16], x[16:32], x[15:16], x[31:32]) for x in (first, second)]
+
+    def compose(za, zp, zc, zr, sem):
+        to_partner(za, zp, sem).wait_recv()
+
+        @pl.loop(1, CHIPS + 1)
+        def _(k):
+            l = chip_peer(k)
+            (s1, r1, p1, h1), (s2, r2, p2, h2) = tile_maps(za, zp, l)
+            zc[l, 0:16, :] = jnp.where(row16 == 15, p1 * p2, p2 * s1 + s2)
+            zc[l, 16:32, :] = jnp.where(
+                row16 == 15, h1 + p1 * p1 * h2, r1 + p1 * (r2 + h2 * s1)
+            )
+
+            @pl.when(l != chip)
+            def _():
+                to_tile(zc.at[l], zr.at[chip], sem.at[2], sem.at[3], tile_of(l)).start()
+
+        zr[chip] = zc[chip]
+
+    def recursion(zr, zo, dc, sem):
+        wait_all(zr, sem.at[3], CHIPS)
+        d = jnp.zeros((16, 128), F32)
         downs = []
-        for s in range(TILES):
+        for s in range(CHIPS):
             downs.append(d)
-            zo[s, 0:8, :] = d
-            d = zr[s, 5:6, :] * d + zr[s, 0:8, :]
-        e = jnp.zeros((8, COLS), F32)
-        for s in reversed(range(TILES)):
-            zo[s, 8:16, :] = e
-            e = zr[s, 5:6, :] * e + (zr[s, 8:16, :] + zr[s, 6:7, :] * downs[s])
-
-        @pl.loop(1, TILES)
+            zo[s, 0:16, :] = d
+            d = zr[s, 15:16, :] * d + zr[s, 0:16, :]
+        e = jnp.zeros((16, 128), F32)
+        for s in reversed(range(CHIPS)):
+            zo[s, 16:32, :] = e
+            e = zr[s, 15:16, :] * e + (zr[s, 16:32, :] + zr[s, 31:32, :] * downs[s])
+
+        @pl.loop(1, CHIPS)
         def _(k):
-            s = tile_peer(k)
-            to_tile(zo.at[s], de.at[t], o_s, o_r, s).start()
-
-        de[t] = zo[t]
+            s = chip_peer(k)
+            to_tile(zo.at[s], dc.at[chip], sem.at[4], sem.at[5], tile_of(s)).start()
+
+        dc[chip] = zo[chip]
+
+    def hand_on(dp, de, sem):
+        return to_tile(dp, de.at[core], sem.at[6], sem.at[7], partner)
+
+    def divide(za, zp, dc, dp, de, sem):
+        wait_all(dc, sem.at[5], CHIPS)
+
+        @pl.loop(0, CHIPS)
+        def _(l):
+            (s1, _r1, p1, _h1), (_s2, r2, p2, h2) = tile_maps(za, zp, l)
+            d1, e2 = dc[l, 0:16, :], dc[l, 16:32, :]
+            d2 = p1 * d1 + s1
+            e1 = p2 * e2 + (r2 + h2 * d2)
+            de[core, l, 0:16, :] = jnp.where(core == 0, d1, d2)
+            de[core, l, 16:32, :] = jnp.where(core == 0, e1, e2)
+            dp[l, 0:16, :] = jnp.where(core == 0, d2, d1)
+            dp[l, 16:32, :] = jnp.where(core == 0, e2, e1)
+
+        hand_on(dp, de, sem).start()
+
+    def carries_sent(za, zp, zc, zo, dp, de, sem):
+        to_partner(za, zp, sem).wait_send()
+        wait_all(zc, sem.at[2], CHIPS)
+        wait_all(zo, sem.at[4], CHIPS)
+        hand_on(dp, de, sem).wait_send()
+
+    sources(lambda l, half: (alpha_of(l, half),), za, 0, LEVELS // 2)
+    to_partner(za, zp, z_sem).start()
 
     lane1 = lax.broadcasted_iota(jnp.int32, (1, 128), 1)
     lane = lax.broadcasted_iota(jnp.int32, (SLOTS, 128), 1)
@@ -369,7 +465,7 @@
             terms = jnp.where(lgroup == (scols[n] & 3), terms, 0.0)
             put = one_hot(sub96 == (srows[n] >> 2))
             both = dot(put, jnp.concatenate(split(terms), axis=1))
-            results.append((both[:, 0:128] + both[:, 128:256]).astype(BF16))
+            results.append(both[:, 0:128] + both[:, 128:256])
         return results
 
     def forward_terms(tiles):
@@ -404,30 +500,52 @@
         scol_v[s] = jnp.where(slot_id < pc_ref[t, s], scol, -1)
         dcol_v[s] = jnp.broadcast_to(turned[:, TILES + s : TILES + s + 1], (SLOTS, 128))
 
-    def back_step(j):
-        tiles = [tile_peer(GROUP * j + 1 + i) for i in range(GROUP)]
+    def off_chip(ch):
+        return to_tile(ss.at[ch], sr.at[chip], ss_s, ss_r, tile_of(ch))
+
+    def core_pair(ch):
+        return to_tile(sf.at[0, ch], sp.at[ch], sp_s, sp_r.at[ch], partner)
+
+    steps = TILES // GROUP
+
+    @pl.loop(0, steps)
+    def _(j):
+        late = j // (steps // 2)
+        chips = [chip_peer(GROUP * (j - steps // 2 * late) + 1 + i) for i in range(GROUP)]
+        tiles = [2 * ch + 1 - core + late * (2 * core - 1) for ch in chips]
         for s in tiles:
             w_load(s).wait()
-        results = back_terms(tiles)
-        for s, r in zip(tiles, results):
-            ss[s] = r
-        for s in tiles:
-
-            @pl.when(s != t)
-            def _():
-                to_tile(ss.at[s], sr.at[t], sp_s, sp_r, s).start()
-
-    steps = TILES // GROUP
-
-    @pl.loop(0, steps)
-    def _(j):
-        back_step(j)
+        for ch, r in zip(chips, back_terms(tiles)):
+            sf[late, ch] = r
+
+        @pl.when(late == 0)
+        def _():
+            for ch in chips:
+                core_pair(ch).start()
+
+        @pl.when(late == 1)
+        def _():
+            for ch in chips:
+                core_pair(ch).wait_recv()
+                ss[ch] = (sf[1, ch] + sp[ch]).astype(BF16)
+
+                @pl.when(ch != chip)
+                def _():
+                    off_chip(ch).start()
+
+        @pl.when(j == steps // 4 - 1)
+        def _():
+            compose(za, zp, zc, zr, z_sem)
 
         @pl.when(j == steps // 2 - 1)
         def _():
-            recursion(zr, zo, de, zs_r, zo_s, zo_r)
-
-    sr[t] = ss[t]
+            recursion(zr, zo, dc, z_sem)
+
+        @pl.when(j == steps - 1)
+        def _():
+            divide(za, zp, dc, dp, de, z_sem)
+
+    sr[chip] = ss[chip]
 
     ax = dx_ref[...]
     posx = lax.broadcasted_iota(jnp.int32, (8, COLS), 1)
@@ -474,7 +592,7 @@
         pltpu.make_async_copy(x, y, out_sem.at[i])
         for i, (x, y) in enumerate(
             [
-                (mt, mt_hbm), (pb, pb_hbm), (qb, qb_hbm), (kk, kk_hbm),
+                (mt, mt_hbm), (pb, pb_hbm), (qb, qb_hbm), (kk.at[:, pl.ds(0, COLS), :], kk_hbm),
                 (back, back_hbm), (de2, de_hbm), (inc_v, inc_hbm),
             ]
         )
@@ -482,9 +600,9 @@
     for x in exports[:4]:
         x.start()
 
-    wait_all(sr, sp_r, TILES)
+    wait_all(sr, ss_r, CHIPS)
     acc = sr[0].astype(F32)
-    for s in range(1, TILES):
+    for s in range(1, CHIPS):
         acc = acc + sr[s].astype(F32)
     bq[...] = acc
     for j in range(3):
@@ -496,12 +614,12 @@
         to_mem(back.at[g], back.at[g], bk_s, bk_r, l).start()
 
     loads[4].wait()
-    wait_all(de, zo_r, TILES)
+    hand_on(dp, de, z_sem).wait_recv()
 
     def partial(l):
         y = smooth(
-            [(alpha_of(l, half),) for half in range(2)], (de[2 * l], de[2 * l + 1]),
-            mt[l], pb[l], qb[l], kk[l], True,
+            [(alpha_of(l, half),) for half in range(2)], (de[0, l], de[1, l]),
+            mt[l], pb[l], qb[l], kk[l, 0:COLS], kk[l, COLS : 2 * COLS],
         )
         acc = jnp.zeros((ROWS, COLS), F32)
         for m in range(2 * HALF):
@@ -526,7 +644,7 @@
         x = pert_v[HALF * half : HALF * half + HALF, l].astype(F32) * back[l][None]
         return split(x.reshape(PACK, COLS))
 
-    sources(weighted, zs2, zr2, zs2_s, zs2_r, 0, 2)
+    sources(weighted, za2, 0, 2)
 
     wait_all(pr, rs_r, LEVELS)
     acc = pr[0]
@@ -537,45 +655,67 @@
         lq[pl.ds(j, ROWS, stride=3), :] = acc[:, 128 * j : 128 * j + 128]
     lows[...] = lq[...].astype(BF16)
 
-    @pl.loop(1, TILES)
+    def low_rows(s):
+        return low.at[s, pl.ds(0, QROWS), :]
+
+    def low_to(s):
+        return to_tile(lows, low_rows(t), lo_s, lo_r.at[t], s)
+
+    def low_on(s):
+        return to_tile(low_rows(s), low_rows(s), lo_f, lo_r.at[s], partner)
+
+    @pl.loop(1, CHIPS)
     def _(k):
-        s = tile_peer(k)
-        to_tile(lows, low.at[t, pl.ds(0, QROWS), :], lo_s, lo_r.at[t], s).start()
+        low_to(tile_of(chip_peer(k))).start()
+
+    low_to(partner).start()
 
     low[t, 0:QROWS, :] = lows[...]
 
-    sources(weighted, zs2, zr2, zs2_s, zs2_r, 2, 4)
+    sources(weighted, za2, 2, 4)
+    to_partner(za2, zp2, z2_sem).start()
 
     inc_v[...] = jnp.zeros((DROWS, 128), F32)
-
-    def forward_step(j):
-        for i in range(GROUP):
-            s = tile_back(GROUP * j + i)
-
-            @pl.when(s != t)
-            def _():
-                to_tile(lows, low.at[s, pl.ds(0, QROWS), :], lo_s, lo_r.at[s], s).wait_recv()
-
-        inc_v[...] += forward_terms([tile_back(GROUP * j + i) for i in range(GROUP)])
 
     @pl.loop(0, steps)
     def _(j):
-        forward_step(j)
+        late = j // (steps // 2)
+        chips = [chip_back(GROUP * (j - steps // 2 * late) + i) for i in range(GROUP)]
+        tiles = [2 * ch + core + late * (1 - 2 * core) for ch in chips]
+        for ch, s in zip(chips, tiles):
+
+            @pl.when((late == 1) | (ch != chip))
+            def _():
+                low_on(s).wait_recv()
+
+            @pl.when((late == 0) & (ch != chip))
+            def _():
+                low_on(s).start()
+
+        inc_v[...] += forward_terms(tiles)
+
+        @pl.when(j == steps // 4 - 1)
+        def _():
+            compose(za2, zp2, zc2, zr2, z2_sem)
 
         @pl.when(j == steps // 2 - 1)
         def _():
-            recursion(zr2, zo2, de2, zs2_r, zo2_s, zo2_r)
-
-    wait_all(de2, zo2_r, TILES)
+            recursion(zr2, zo2, dc2, z2_sem)
+
+        @pl.when(j == 3 * steps // 4 - 1)
+        def _():
+            divide(za2, zp2, dc2, dp2, de2, z2_sem)
+
+    hand_on(dp2, de2, z2_sem).wait_recv()
     exports[5].start()
     exports[6].start()
 
-    wait_all(zs, zs_s, TILES)
-    wait_all(zo, zo_s, TILES)
-    wait_all(zs2, zs2_s, TILES)
-    wait_all(zo2, zo2_s, TILES)
-    wait_all(ss, sp_s, TILES)
-    wait_all(sr, lo_s, TILES)
+    carries_sent(za, zp, zc, zo, dp, de, z_sem)
+    carries_sent(za2, zp2, zc2, zo2, dp2, de2, z2_sem)
+    pltpu.make_async_copy(sp, sp, sp_s).wait()
+    wait_all(ss, ss_s, CHIPS)
+    pltpu.make_async_copy(sr, sr, lo_s).wait()
+    wait_all(sr, lo_f, CHIPS)
     wait_all(ps, rs_s, LEVELS)
     wait_all(back, bk_s, LEVELS)
     for x in exports:
@@ -591,7 +731,9 @@
     smem = pl.BlockSpec(memory_space=pltpu.SMEM)
     dma = pltpu.SemaphoreType.DMA
     V = pltpu.VMEM
-    zbuf = V((TILES, 16, COLS), F32)
+    zbuf = V((CHIPS, 32, 128), F32)
+    zpair = V((2, CHIPS, 32, 128), F32)
+    zall = [zpair, *[zbuf] * 6, zpair]
     scratch = [
         V((2 * HALF, LEVELS, ROWS, COLS), BF16),
         V((2 * HALF, LEVELS, ROWS, COLS), BF16),
@@ -606,13 +748,15 @@
         V((LEVELS, 8, COLS), F32),
         V((LEVELS, PACK, 512), BF16),
         V((LEVELS, 32, PACK), BF16),
-        V((LEVELS, 16, COLS), F32),
         V((LEVELS, ROWS, 128), F32),
         V((LEVELS, ROWS, 128), F32),
         V((LEVELS, 2 * COLS, COLS), BF16),
-        *[zbuf] * 8,
-        V((TILES, QROWS, 128), BF16),
-        V((TILES, QROWS, 128), BF16),
+        *zall,
+        *zall,
+        V((2, CHIPS, QROWS, 128), F32),
+        V((CHIPS, QROWS, 128), F32),
+        V((CHIPS, QROWS, 128), BF16),
+        V((CHIPS, QROWS, 128), BF16),
         V((QROWS, 128), F32),
         V((LEVELS, ROWS, COLS), F32),
         V((LEVELS, ROWS, COLS), F32),
@@ -626,8 +770,11 @@
         dma((5,)),
         dma((TILES,)),
         dma((7,)),
-        *[dma] * 12,
+        dma((8,)),
+        dma((8,)),
         dma,
+        dma((CHIPS,)),
+        *[dma] * 6,
         dma((TILES,)),
         dma,
         dma,
@@ -638,11 +785,11 @@
         out_shape=(
             shape((DROWS, 128), F32),
             shape((LEVELS, ROWS, COLS), F32),
-            shape((TILES, 16, COLS), F32),
+            shape((2, CHIPS, 32, 128), F32),
             shape((LEVELS, PACK, 512), BF16),
             shape((LEVELS, ROWS, 128), F32),
             shape((LEVELS, ROWS, 128), F32),
-            shape((LEVELS, 2 * COLS, COLS), BF16),
+            shape((LEVELS, COLS, COLS), BF16),
         ),
         in_specs=[any_spec, any_spec, any_spec, vmem, vmem, smem, any_spec, smem, any_spec, any_spec],
         out_specs=(any_spec,) * 7,
@@ -658,29 +805,27 @@
         interp_weight, pair_count, src_index, dst_index,
     )
 
-    def level(*block):
-        return pl.BlockSpec(block, lambda l: (l,) + (0,) * (len(block) - 1))
-
-    member_block = pl.BlockSpec((2 * HALF, 1, ROWS, COLS), lambda l: (0, l, 0, 0))
+    members_shape = (2 * HALF, LEVELS, ROWS, COLS)
     return pl.pallas_call(
         grad_kernel,
-        grid=(LEVELS,),
         out_shape=(shape((1, DROWS * 128), F32), shape(alpha.shape, F32)),
-        in_specs=[
-            smem,
-            member_block,
-            level(1, ROWS, COLS),
-            level(2, 16, COLS),
-            level(1, PACK, 512),
-            level(1, ROWS, 128),
-            level(1, ROWS, 128),
-            level(1, 2 * COLS, COLS),
-            pl.BlockSpec((DROWS, 128), lambda l: (0, 0)),
+        in_specs=[smem, *[any_spec] * 7, vmem],
+        out_specs=(vmem, any_spec),
+        scratch_shapes=[
+            V(members_shape, BF16),
+            V((LEVELS, ROWS, COLS), F32),
+            V((2, CHIPS, 32, 128), F32),
+            V((LEVELS, PACK, 512), BF16),
+            V((LEVELS, ROWS, 128), F32),
+            V((LEVELS, ROWS, 128), F32),
+            V((LEVELS, COLS, COLS), BF16),
+            V(members_shape, F32),
+            dma((7, LEVELS)),
+            dma((LEVELS,)),
         ],
-        out_specs=(pl.BlockSpec((1, DROWS * 128), lambda l: (0, 0)), member_block),
         compiler_params=pltpu.CompilerParams(vmem_limit_bytes=60 * 1024 * 1024),
         cost_estimate=pl.CostEstimate(
-            flops=3_500_000_000, bytes_accessed=13_000_000, transcendentals=0
+            flops=3_500_000_000, bytes_accessed=11_000_000, transcendentals=0
         ),
     )(group_members, perturbation, *rest, inc)
 

time: 70.1 us -> 70.7 us (level)
    pallas_call x1, Pallas kernels: 58.9 us -> 60.1 us  [shards(): pl.pallas_call(kernel, out_shape=(shape((DROWS, 128), F32), shape((LEVELS...]
where the time goes in v3:
time: 70.7 us; the launch traced here: 70.3 us
  Pallas kernels  69.6 us (98%)
    pallas_call x1, Pallas kernels, shards(): pl.pallas_call(kernel, out_shape=(shape((DROWS, 128), F32), shape((LEVELS...  60.1 us
    pallas_call x1, Pallas kernels, shards(): pl.pallas_call(grad_kernel, out_shape=(shape((1, DROWS * 128), F32), shap...  9.5 us

profile of v3, /device:TPU:1, one launch (start us, length us, event | category | flops | bytes accessed | tf_op | source)
XLA Modules:
  0.0 70.3 jit_solution(16872126016361066877)
XLA Ops:
  0.6 60.1 %shard_map.113 = (f32[384,128]{1,0:T(8,128)}, f32[8,32,384]{2,1,0:T(8,128)}, f32[2,8,32,128]{3,2,1,0:T(8,128)}, bf16[8,160,512]{2,1,0:T(8,128)(2,1)}, f32[8,32,1...) custom-call(bf16[10,8,32,384]{3,2,1,0:T(8,128)(2,1)} %alpha_hbm.1, ...), custom_call_target="tpu_custom_call" | custom-call | flops 8999999488 | bytes 29000000 | tf_op jit(solution)/shard_map/pallas_call | solution.py:783
  60.8 9.5 %shard_map.114 = (f32[1,49152]{1,0:T(1,128)}, f32[10,8,32,384]{3,2,1,0:T(8,128)}) custom-call(s32[8]{0:T(128)} %gm_ref.3, bf16[10,8,32,384]{3,2,1,0:T(8,128)(2,1)} %pert_hbm.3, f32[8,32,384]{2,1,0:T(8,128)} %get-tuple-element.9.back_hbm, f32[2,8,32,128]{3,2,1,0:T(8,128)} %get-tuple-element.10.de_hbm, bf16[8,160,512]{2,1,0:T(8,128)(2,1)} %get-tuple-element.11.mt_hbm, ...), custom_call_target="tpu_custom_call" | custom-call | flops 3500000000 | bytes 11000000 | tf_op jit(solution)/shard_map/pallas_call | solution.py:809

commit v4 on v3

--- a/solution.py
+++ b/solution.py
@@ -132,7 +132,7 @@
             x.wait()
         fields = []
         for half in range(2):
-            x = pert_v[HALF * half : HALF * half + HALF, l].astype(F32) * back_v[l][None]
+            x = pert_v[HALF * half : HALF * half + HALF, l].astype(F32) * back_v[l].astype(F32)[None]
             fields.append(split(x.reshape(PACK, COLS)))
         y = smooth(fields, (de_v[0, l], de_v[1, l]), mt_v[l], pb_v[l], qb_v[l], kk_v[l])
         for m in range(2 * HALF):
@@ -527,7 +527,7 @@
         def _():
             for ch in chips:
                 core_pair(ch).wait_recv()
-                ss[ch] = (sf[1, ch] + sp[ch]).astype(BF16)
+                ss[ch] = sf[1, ch] + sp[ch]
 
                 @pl.when(ch != chip)
                 def _():
@@ -601,12 +601,12 @@
         x.start()
 
     wait_all(sr, ss_r, CHIPS)
-    acc = sr[0].astype(F32)
+    acc = sr[0]
     for s in range(1, CHIPS):
-        acc = acc + sr[s].astype(F32)
+        acc = acc + sr[s]
     bq[...] = acc
     for j in range(3):
-        back[g, :, 128 * j : 128 * j + 128] = bq[pl.ds(j, ROWS, stride=3), :]
+        back[g, :, 128 * j : 128 * j + 128] = bq[pl.ds(j, ROWS, stride=3), :].astype(BF16)
 
     @pl.loop(1, LEVELS)
     def _(k):
@@ -641,7 +641,7 @@
     exports[4].start()
 
     def weighted(l, half):
-        x = pert_v[HALF * half : HALF * half + HALF, l].astype(F32) * back[l][None]
+        x = pert_v[HALF * half : HALF * half + HALF, l].astype(F32) * back[l].astype(F32)[None]
         return split(x.reshape(PACK, COLS))
 
     sources(weighted, za2, 0, 2)
@@ -679,16 +679,20 @@
 
     @pl.loop(0, steps)
     def _(j):
-        late = j // (steps // 2)
-        chips = [chip_back(GROUP * (j - steps // 2 * late) + i) for i in range(GROUP)]
-        tiles = [2 * ch + core + late * (1 - 2 * core) for ch in chips]
-        for ch, s in zip(chips, tiles):
-
-            @pl.when((late == 1) | (ch != chip))
+        tiles = []
+        for i in range(GROUP):
+            n = GROUP * j + i
+            afar = (n + TILES - 2) // TILES
+            late = n // (CHIPS + 1)
+            ch = chip_back(afar * (n - 1 - (CHIPS - 1) * late))
+            s = 2 * ch + core + (late + (1 - afar) * lax.rem(n, 2)) * (1 - 2 * core)
+            tiles.append(s)
+
+            @pl.when(n > 0)
             def _():
                 low_on(s).wait_recv()
 
-            @pl.when((late == 0) & (ch != chip))
+            @pl.when((afar == 1) & (late == 0))
             def _():
                 low_on(s).start()
 
@@ -714,8 +718,10 @@
     carries_sent(za2, zp2, zc2, zo2, dp2, de2, z2_sem)
     pltpu.make_async_copy(sp, sp, sp_s).wait()
     wait_all(ss, ss_s, CHIPS)
-    pltpu.make_async_copy(sr, sr, lo_s).wait()
-    wait_all(sr, lo_f, CHIPS)
+    lows8 = low.at[pl.ds(0, CHIPS), pl.ds(0, QROWS), :]
+    pltpu.make_async_copy(lows8, lows8, lo_s).wait()
+    lows7 = low.at[pl.ds(0, CHIPS - 1), pl.ds(0, QROWS), :]
+    pltpu.make_async_copy(lows7, lows7, lo_f).wait()
     wait_all(ps, rs_s, LEVELS)
     wait_all(back, bk_s, LEVELS)
     for x in exports:
@@ -755,10 +761,10 @@
         *zall,
         V((2, CHIPS, QROWS, 128), F32),
         V((CHIPS, QROWS, 128), F32),
-        V((CHIPS, QROWS, 128), BF16),
-        V((CHIPS, QROWS, 128), BF16),
+        V((CHIPS, QROWS, 128), F32),
+        V((CHIPS, QROWS, 128), F32),
         V((QROWS, 128), F32),
-        V((LEVELS, ROWS, COLS), F32),
+        V((LEVELS, ROWS, COLS), BF16),
         V((LEVELS, ROWS, COLS), F32),
         V((LEVELS, ROWS, COLS), F32),
         V((QROWS, 128), F32),
@@ -784,7 +790,7 @@
         kernel,
         out_shape=(
             shape((DROWS, 128), F32),
-            shape((LEVELS, ROWS, COLS), F32),
+            shape((LEVELS, ROWS, COLS), BF16),
             shape((2, CHIPS, 32, 128), F32),
             shape((LEVELS, PACK, 512), BF16),
             shape((LEVELS, ROWS, 128), F32),
@@ -813,7 +819,7 @@
         out_specs=(vmem, any_spec),
         scratch_shapes=[
             V(members_shape, BF16),
-            V((LEVELS, ROWS, COLS), F32),
+            V((LEVELS, ROWS, COLS), BF16),
             V((2, CHIPS, 32, 128), F32),
             V((LEVELS, PACK, 512), BF16),
             V((LEVELS, ROWS, 128), F32),

time: 70.7 us -> 68.2 us (0.965)
  Pallas kernels: 69.6 us -> 67 us
    pallas_call x1, Pallas kernels: 60.1 us -> 57.5 us  [shards(): pl.pallas_call(kernel, out_shape=(shape((DROWS, 128), F32), shape((LEVELS...]
where the time goes in v4:
time: 68.2 us; the launch traced here: 67.7 us
  Pallas kernels  67 us (98%)
    pallas_call x1, Pallas kernels, shards(): pl.pallas_call(kernel, out_shape=(shape((DROWS, 128), F32), shape((LEVELS...  57.5 us
    pallas_call x1, Pallas kernels, shards(): pl.pallas_call(grad_kernel, out_shape=(shape((1, DROWS * 128), F32), shap...  9.52 us

profile of v4, /device:TPU:1, one launch (start us, length us, event | category | flops | bytes accessed | tf_op | source)
XLA Modules:
  0.0 67.7 jit_solution(5773114937609616890)
XLA Ops:
  0.6 57.5 %shard_map.113 = (f32[384,128]{1,0:T(8,128)}, bf16[8,32,384]{2,1,0:T(8,128)(2,1)}, f32[2,8,32,128]{3,2,1,0:T(8,128)}, bf16[8,160,512]{2,1,0:T(8,128)(2,1)}, f32[...) custom-call(bf16[10,8,32,384]{3,2,1,0:T(8,128)(2,1)} %alpha_hbm.1, ...), custom_call_target="tpu_custom_call" | custom-call | flops 8999999488 | bytes 29000000 | tf_op jit(solution)/shard_map/pallas_call | solution.py:789
  58.2 9.5 %shard_map.114 = (f32[1,49152]{1,0:T(1,128)}, f32[10,8,32,384]{3,2,1,0:T(8,128)}) custom-call(s32[8]{0:T(128)} %gm_ref.3, bf16[10,8,32,384]{3,2,1,0:T(8,128)(2,1)} %pert_hbm.3, bf16[8,32,384]{2,1,0:T(8,128)(2,1)} %get-tuple-element.9.back_hbm, f32[2,8,32,128]{3,2,1,0:T(8,128)} %get-tuple-element.10.de_hbm, bf16[8,160,512]{2,1,0:T(8,128)(2,1)} %get-tuple-element.11.mt_hbm, ...), custom_call_target="tpu_custom_call" | custom-call | flops 3500000000 | bytes 11000000 | tf_op jit(solution)/shard_map/pallas_call | solution.py:815

commit v5 on v4

--- a/solution.py
+++ b/solution.py
@@ -94,24 +94,26 @@
 def grad_kernel(
     gm_ref, pert_hbm, back_hbm, de_hbm, mt_hbm, pb_hbm, qb_hbm, kk_hbm, inc_ref,
     inc_out, grad_hbm,
-    pert_v, back_v, de_v, mt_v, pb_v, qb_v, kk_v, out_v, in_sem, out_sem,
+    pert_v, back_v, de_v, mt_v, pb_v, qb_v, kk_v, out_v, whole_sem, in_sem, out_sem,
 ):
+    whole = [
+        pltpu.make_async_copy(a, b, whole_sem.at[i])
+        for i, (a, b) in enumerate(
+            [(back_hbm, back_v), (de_hbm, de_v), (pb_hbm, pb_v), (qb_hbm, qb_v), (mt_hbm, mt_v)]
+        )
+    ]
+
     def loads(l):
-        pairs = [
-            (pert_hbm.at[:, l], pert_v.at[:, l]),
-            (back_hbm.at[l], back_v.at[l]),
-            (de_hbm.at[:, l], de_v.at[:, l]),
-            (mt_hbm.at[l], mt_v.at[l]),
-            (pb_hbm.at[l], pb_v.at[l]),
-            (qb_hbm.at[l], qb_v.at[l]),
-            (kk_hbm.at[l], kk_v.at[l]),
-        ]
         return [
-            pltpu.make_async_copy(a, b, in_sem.at[i, l]) for i, (a, b) in enumerate(pairs)
+            pltpu.make_async_copy(pert_hbm.at[:, l], pert_v.at[:, l], in_sem.at[0, l]),
+            pltpu.make_async_copy(kk_hbm.at[l], kk_v.at[l], in_sem.at[1, l]),
         ]
 
     def store(l):
         return pltpu.make_async_copy(out_v.at[:, l], grad_hbm.at[:, l], out_sem.at[l])
+
+    for x in whole:
+        x.start()
 
     @pl.loop(0, LEVELS)
     def _(l):
@@ -125,6 +127,9 @@
         x = inc_ref[pl.ds(pl.multiple_of(8 * i, 8), 8), :]
         for r in range(8):
             inc_out[0:1, pl.ds(pl.multiple_of(1024 * i + 128 * r, 128), 128)] = x[r : r + 1, :]
+
+    for x in whole:
+        x.wait()
 
     @pl.loop(0, LEVELS)
     def _(l):
@@ -149,7 +154,7 @@
     inc_hbm, back_hbm, de_hbm, mt_hbm, pb_hbm, qb_hbm, kk_hbm,
     alpha_v, pert_v, cot_raw, cot_v, w_v, src_v, dst_v,
     rep_v, yt, ytail, xt, mt, zf, pb, qb, kk,
-    za, zp, zc, zr, zo, dc, dp, de, za2, zp2, zc2, zr2, zo2, dc2, dp2, de2,
+    za, zr, zo, de, za2, zr2, zo2, de2,
     sf, sp, ss, sr, bq, back, ps, pr, lq, low, lows, inc_v, scol_v, dcol_v,
     in_sem, w_sem, out_sem, z_sem, z2_sem,
     sp_s, sp_r, ss_s, ss_r, rs_s, rs_r, lo_s, lo_f, lo_r, bk_s, bk_r,
@@ -210,12 +215,10 @@
 
     barrier = pltpu.get_barrier_semaphore()
 
-    pl.semaphore_signal(barrier, inc=1, device_id={"tile": partner}, device_id_type=MESH)
-
-    @pl.loop(1, CHIPS)
+    @pl.loop(1, TILES)
     def _(k):
         pl.semaphore_signal(
-            barrier, inc=1, device_id={"tile": tile_of(chip_peer(k))}, device_id_type=MESH
+            barrier, inc=1, device_id={"tile": lax.rem(t + k, TILES)}, device_id_type=MESH
         )
 
     @pl.loop(1, LEVELS)
@@ -286,7 +289,7 @@
         cot_v[pl.ds(pl.multiple_of(16 * i, 16), 16), :] = jnp.concatenate(rows, axis=0).astype(BF16)
 
     loads[0].wait()
-    pl.semaphore_wait(barrier, 1 + CHIPS - 1 + LEVELS - 1)
+    pl.semaphore_wait(barrier, TILES - 1 + LEVELS - 1)
 
     def alpha_of(l, half):
         return alpha_v[HALF * half : HALF * half + HALF, l].reshape(PACK, COLS)
@@ -298,12 +301,12 @@
             z = z + dot(zf[l, 0:16, :], lo)
         return z
 
-    def sources(field, za, first, last):
+    def sources(field, za, zr, sem, first, last):
         @pl.loop(first, last)
         def _(k):
             found = []
             for i in range(2):
-                l = 2 * k + i
+                l = lax.rem(chip + 2 * k + i + 1, LEVELS)
                 for half in range(2):
                     found.append((half, l, source(l, *field(l, half))))
             for half, l, z in found:
@@ -313,84 +316,43 @@
                     za[half, l, 16 + HALF * j : 16 + HALF * j + HALF, :] = part[8 : 8 + HALF]
                 za[half, l, 15:16, :] = ytail[l, 0:1, 0:128]
                 za[half, l, 31:32, :] = ytail[l, 1:2, 0:128]
-
-    def to_partner(za, zp, sem):
-        other = za.at[1 - core]
-        return to_tile(other, zp, sem.at[0], sem.at[1], partner)
-
-    row16 = lax.broadcasted_iota(jnp.int32, (16, 128), 0)
-
-    def tile_maps(za, zp, l):
-        own, theirs = za[core, l], zp[l]
-        first = jnp.where(core == 0, own, theirs)
-        second = jnp.where(core == 0, theirs, own)
-        return [(x[0:16], x[16:32], x[15:16], x[31:32]) for x in (first, second)]
-
-    def compose(za, zp, zc, zr, sem):
-        to_partner(za, zp, sem).wait_recv()
-
-        @pl.loop(1, CHIPS + 1)
-        def _(k):
-            l = chip_peer(k)
-            (s1, r1, p1, h1), (s2, r2, p2, h2) = tile_maps(za, zp, l)
-            zc[l, 0:16, :] = jnp.where(row16 == 15, p1 * p2, p2 * s1 + s2)
-            zc[l, 16:32, :] = jnp.where(
-                row16 == 15, h1 + p1 * p1 * h2, r1 + p1 * (r2 + h2 * s1)
-            )
-
-            @pl.when(l != chip)
-            def _():
-                to_tile(zc.at[l], zr.at[chip], sem.at[2], sem.at[3], tile_of(l)).start()
-
-        zr[chip] = zc[chip]
-
-    def recursion(zr, zo, dc, sem):
-        wait_all(zr, sem.at[3], CHIPS)
+            for half, l, _z in found:
+
+                @pl.when(2 * l + half != t)
+                def _():
+                    to_tile(za.at[half, l], zr.at[t], sem.at[0], sem.at[1], 2 * l + half).start()
+
+        if last == LEVELS // 2:
+            zr[t] = za[core, chip]
+
+    def recursion(zr, zo, de, sem):
+        wait_all(zr, sem.at[1], TILES)
         d = jnp.zeros((16, 128), F32)
         downs = []
-        for s in range(CHIPS):
+        for s in range(TILES):
             downs.append(d)
             zo[s, 0:16, :] = d
             d = zr[s, 15:16, :] * d + zr[s, 0:16, :]
         e = jnp.zeros((16, 128), F32)
-        for s in reversed(range(CHIPS)):
+        for s in reversed(range(TILES)):
             zo[s, 16:32, :] = e
             e = zr[s, 15:16, :] * e + (zr[s, 16:32, :] + zr[s, 31:32, :] * downs[s])
 
-        @pl.loop(1, CHIPS)
+        @pl.loop(1, TILES)
         def _(k):
-            s = chip_peer(k)
-            to_tile(zo.at[s], dc.at[chip], sem.at[4], sem.at[5], tile_of(s)).start()
-
-        dc[chip] = zo[chip]
-
-    def hand_on(dp, de, sem):
-        return to_tile(dp, de.at[core], sem.at[6], sem.at[7], partner)
-
-    def divide(za, zp, dc, dp, de, sem):
-        wait_all(dc, sem.at[5], CHIPS)
-
-        @pl.loop(0, CHIPS)
-        def _(l):
-            (s1, _r1, p1, _h1), (_s2, r2, p2, h2) = tile_maps(za, zp, l)
-            d1, e2 = dc[l, 0:16, :], dc[l, 16:32, :]
-            d2 = p1 * d1 + s1
-            e1 = p2 * e2 + (r2 + h2 * d2)
-            de[core, l, 0:16, :] = jnp.where(core == 0, d1, d2)
-            de[core, l, 16:32, :] = jnp.where(core == 0, e1, e2)
-            dp[l, 0:16, :] = jnp.where(core == 0, d2, d1)
-            dp[l, 16:32, :] = jnp.where(core == 0, e2, e1)
-
-        hand_on(dp, de, sem).start()
-
-    def carries_sent(za, zp, zc, zo, dp, de, sem):
-        to_partner(za, zp, sem).wait_send()
-        wait_all(zc, sem.at[2], CHIPS)
-        wait_all(zo, sem.at[4], CHIPS)
-        hand_on(dp, de, sem).wait_send()
-
-    sources(lambda l, half: (alpha_of(l, half),), za, 0, LEVELS // 2)
-    to_partner(za, zp, z_sem).start()
+            s = lax.rem(t + k, TILES)
+            to_tile(zo.at[s], de.at[core, chip], sem.at[2], sem.at[3], s).start()
+
+        de[core, chip] = zo[t]
+
+    def carries_in(zo, sem):
+        wait_all(zo, sem.at[3], TILES)
+
+    def carries_sent(zo, sem):
+        wait_all(zo, sem.at[0], TILES)
+        wait_all(zo, sem.at[2], TILES)
+
+    sources(lambda l, half: (alpha_of(l, half),), za, zr, z_sem, 0, LEVELS // 2)
 
     lane1 = lax.broadcasted_iota(jnp.int32, (1, 128), 1)
     lane = lax.broadcasted_iota(jnp.int32, (SLOTS, 128), 1)
@@ -533,17 +495,9 @@
                 def _():
                     off_chip(ch).start()
 
-        @pl.when(j == steps // 4 - 1)
-        def _():
-            compose(za, zp, zc, zr, z_sem)
-
         @pl.when(j == steps // 2 - 1)
         def _():
-            recursion(zr, zo, dc, z_sem)
-
-        @pl.when(j == steps - 1)
-        def _():
-            divide(za, zp, dc, dp, de, z_sem)
+            recursion(zr, zo, de, z_sem)
 
     sr[chip] = ss[chip]
 
@@ -614,7 +568,7 @@
         to_mem(back.at[g], back.at[g], bk_s, bk_r, l).start()
 
     loads[4].wait()
-    hand_on(dp, de, z_sem).wait_recv()
+    carries_in(zo, z_sem)
 
     def partial(l):
         y = smooth(
@@ -644,7 +598,7 @@
         x = pert_v[HALF * half : HALF * half + HALF, l].astype(F32) * back[l].astype(F32)[None]
         return split(x.reshape(PACK, COLS))
 
-    sources(weighted, za2, 0, 2)
+    sources(weighted, za2, zr2, z2_sem, 0, 2)
 
     wait_all(pr, rs_r, LEVELS)
     acc = pr[0]
@@ -672,8 +626,7 @@
 
     low[t, 0:QROWS, :] = lows[...]
 
-    sources(weighted, za2, 2, 4)
-    to_partner(za2, zp2, z2_sem).start()
+    sources(weighted, za2, zr2, z2_sem, 2, 4)
 
     inc_v[...] = jnp.zeros((DROWS, 128), F32)
 
@@ -698,24 +651,16 @@
 
         inc_v[...] += forward_terms(tiles)
 
-        @pl.when(j == steps // 4 - 1)
-        def _():
-            compose(za2, zp2, zc2, zr2, z2_sem)
-
         @pl.when(j == steps // 2 - 1)
         def _():
-            recursion(zr2, zo2, dc2, z2_sem)
-
-        @pl.when(j == 3 * steps // 4 - 1)
-        def _():
-            divide(za2, zp2, dc2, dp2, de2, z2_sem)
-
-    hand_on(dp2, de2, z2_sem).wait_recv()
+            recursion(zr2, zo2, de2, z2_sem)
+
+    exports[6].start()
+    carries_in(zo2, z2_sem)
     exports[5].start()
-    exports[6].start()
-
-    carries_sent(za, zp, zc, zo, dp, de, z_sem)
-    carries_sent(za2, zp2, zc2, zo2, dp2, de2, z2_sem)
+
+    carries_sent(zo, z_sem)
+    carries_sent(zo2, z2_sem)
     pltpu.make_async_copy(sp, sp, sp_s).wait()
     wait_all(ss, ss_s, CHIPS)
     lows8 = low.at[pl.ds(0, CHIPS), pl.ds(0, QROWS), :]
@@ -737,9 +682,9 @@
     smem = pl.BlockSpec(memory_space=pltpu.SMEM)
     dma = pltpu.SemaphoreType.DMA
     V = pltpu.VMEM
-    zbuf = V((CHIPS, 32, 128), F32)
+    zbuf = V((TILES, 32, 128), F32)
     zpair = V((2, CHIPS, 32, 128), F32)
-    zall = [zpair, *[zbuf] * 6, zpair]
+    zall = [zpair, zbuf, zbuf, zpair]
     scratch = [
         V((2 * HALF, LEVELS, ROWS, COLS), BF16),
         V((2 * HALF, LEVELS, ROWS, COLS), BF16),
@@ -776,8 +721,8 @@
         dma((5,)),
         dma((TILES,)),
         dma((7,)),
-        dma((8,)),
-        dma((8,)),
+        dma((4,)),
+        dma((4,)),
         dma,
         dma((CHIPS,)),
         *[dma] * 6,
@@ -826,7 +771,8 @@
             V((LEVELS, ROWS, 128), F32),
             V((LEVELS, COLS, COLS), BF16),
             V(members_shape, F32),
-            dma((7, LEVELS)),
+            dma((5,)),
+            dma((2, LEVELS)),
             dma((LEVELS,)),
         ],
         compiler_params=pltpu.CompilerParams(vmem_limit_bytes=60 * 1024 * 1024),

time: 68.2 us -> 63.4 us (0.930)
  Pallas kernels: 67 us -> 62.5 us
    pallas_call x1, Pallas kernels: 57.5 us -> 52.8 us  [shards(): pl.pallas_call(kernel, out_shape=(shape((DROWS, 128), F32), shape((LEVELS...]
where the time goes in v5:
time: 63.4 us; the launch traced here: 63.1 us
  Pallas kernels  62.5 us (99%)
  between operations  0.64 us (1%)
    pallas_call x1, Pallas kernels, shards(): pl.pallas_call(kernel, out_shape=(shape((DROWS, 128), F32), shape((LEVELS...  52.8 us
    pallas_call x1, Pallas kernels, shards(): pl.pallas_call(grad_kernel, out_shape=(shape((1, DROWS * 128), F32), shap...  9.65 us

profile of v5, /device:TPU:1, one launch (start us, length us, event | category | flops | bytes accessed | tf_op | source)
XLA Modules:
  0.0 63.1 jit_solution(16733362249153059633)
XLA Ops:
  0.6 52.8 %shard_map.113 = (f32[384,128]{1,0:T(8,128)}, bf16[8,32,384]{2,1,0:T(8,128)(2,1)}, f32[2,8,32,128]{3,2,1,0:T(8,128)}, bf16[8,160,512]{2,1,0:T(8,128)(2,1)}, f32[...) custom-call(bf16[10,8,32,384]{3,2,1,0:T(8,128)(2,1)} %alpha_hbm.1, ...), custom_call_target="tpu_custom_call" | custom-call | flops 8999999488 | bytes 29000000 | tf_op jit(solution)/shard_map/pallas_call | solution.py:734
  53.5 9.7 %shard_map.114 = (f32[1,49152]{1,0:T(1,128)}, f32[10,8,32,384]{3,2,1,0:T(8,128)}) custom-call(s32[8]{0:T(128)} %gm_ref.3, bf16[10,8,32,384]{3,2,1,0:T(8,128)(2,1)} %pert_hbm.3, bf16[8,32,384]{2,1,0:T(8,128)(2,1)} %get-tuple-element.9.back_hbm, f32[2,8,32,128]{3,2,1,0:T(8,128)} %get-tuple-element.10.de_hbm, bf16[8,160,512]{2,1,0:T(8,128)(2,1)} %get-tuple-element.11.mt_hbm, ...), custom_call_target="tpu_custom_call" | custom-call | flops 3500000000 | bytes 11000000 | tf_op jit(solution)/shard_map/pallas_call | solution.py:760

commit v6 on v5

--- a/solution.py
+++ b/solution.py
@@ -99,7 +99,7 @@
     whole = [
         pltpu.make_async_copy(a, b, whole_sem.at[i])
         for i, (a, b) in enumerate(
-            [(back_hbm, back_v), (de_hbm, de_v), (pb_hbm, pb_v), (qb_hbm, qb_v), (mt_hbm, mt_v)]
+            [(back_hbm, back_v), (de_hbm, de_v), (pb_hbm, pb_v), (qb_hbm, qb_v)]
         )
     ]
 
@@ -107,6 +107,7 @@
         return [
             pltpu.make_async_copy(pert_hbm.at[:, l], pert_v.at[:, l], in_sem.at[0, l]),
             pltpu.make_async_copy(kk_hbm.at[l], kk_v.at[l], in_sem.at[1, l]),
+            pltpu.make_async_copy(mt_hbm.at[l], mt_v.at[l], in_sem.at[2, l]),
         ]
 
     def store(l):
@@ -205,13 +206,15 @@
     def w_load(s):
         return pltpu.make_async_copy(w_hbm.at[0, s], w_v.at[s], w_sem.at[s])
 
-    for c in loads:
+    for c in loads[:4]:
         c.start()
 
     @pl.loop(0, TILES)
     def _(i):
         late = i // CHIPS
         w_load(2 * chip_peer(i - CHIPS * late + 1) + 1 - core + late * (2 * core - 1)).start()
+
+    loads[4].start()
 
     barrier = pltpu.get_barrier_semaphore()
 
@@ -276,18 +279,6 @@
         pb[l] = jnp.broadcast_to(col(3), (ROWS, 128))
         qb[l] = jnp.broadcast_to(col(4), (ROWS, 128))
 
-    low[:, QROWS:128, :] = jnp.zeros((TILES, 128 - QROWS, 128), BF16)
-
-    loads[1].wait()
-
-    @pl.loop(0, DROWS // 16)
-    def _(i):
-        rows = [
-            cot_raw[:, pl.ds(pl.multiple_of(2048 * i + 128 * r, 128), 128)].astype(F32)
-            for r in range(16)
-        ]
-        cot_v[pl.ds(pl.multiple_of(16 * i, 16), 16), :] = jnp.concatenate(rows, axis=0).astype(BF16)
-
     loads[0].wait()
     pl.semaphore_wait(barrier, TILES - 1 + LEVELS - 1)
 
@@ -353,6 +344,18 @@
         wait_all(zo, sem.at[2], TILES)
 
     sources(lambda l, half: (alpha_of(l, half),), za, zr, z_sem, 0, LEVELS // 2)
+
+    low[:, QROWS:128, :] = jnp.zeros((TILES, 128 - QROWS, 128), BF16)
+
+    loads[1].wait()
+
+    @pl.loop(0, DROWS // 16)
+    def _(i):
+        rows = [
+            cot_raw[:, pl.ds(pl.multiple_of(2048 * i + 128 * r, 128), 128)].astype(F32)
+            for r in range(16)
+        ]
+        cot_v[pl.ds(pl.multiple_of(16 * i, 16), 16), :] = jnp.concatenate(rows, axis=0).astype(BF16)
 
     lane1 = lax.broadcasted_iota(jnp.int32, (1, 128), 1)
     lane = lax.broadcasted_iota(jnp.int32, (SLOTS, 128), 1)
@@ -495,7 +498,7 @@
                 def _():
                     off_chip(ch).start()
 
-        @pl.when(j == steps // 2 - 1)
+        @pl.when(j == steps // 2)
         def _():
             recursion(zr, zo, de, z_sem)
 
@@ -771,8 +774,8 @@
             V((LEVELS, ROWS, 128), F32),
             V((LEVELS, COLS, COLS), BF16),
             V(members_shape, F32),
-            dma((5,)),
-            dma((2, LEVELS)),
+            dma((4,)),
+            dma((3, LEVELS)),
             dma((LEVELS,)),
         ],
         compiler_params=pltpu.CompilerParams(vmem_limit_bytes=60 * 1024 * 1024),

time: 63.4 us -> 65 us (1.025)
  Pallas kernels: 62.5 us -> 63.5 us
    pallas_call x1, Pallas kernels: 52.8 us -> 54.1 us  [shards(): pl.pallas_call(kernel, out_shape=(shape((DROWS, 128), F32), shape((LEVELS...]
where the time goes in v6:
time: 65 us; the launch traced here: 64.1 us
  Pallas kernels  63.5 us (98%)
    pallas_call x1, Pallas kernels, shards(): pl.pallas_call(kernel, out_shape=(shape((DROWS, 128), F32), shape((LEVELS...  54.1 us
    pallas_call x1, Pallas kernels, shards(): pl.pallas_call(grad_kernel, out_shape=(shape((1, DROWS * 128), F32), shap...  9.36 us

profile of v6, /device:TPU:1, one launch (start us, length us, event | category | flops | bytes accessed | tf_op | source)
XLA Modules:
  0.0 64.1 jit_solution(12510956055363616646)
XLA Ops:
  0.6 54.1 %shard_map.113 = (f32[384,128]{1,0:T(8,128)}, bf16[8,32,384]{2,1,0:T(8,128)(2,1)}, f32[2,8,32,128]{3,2,1,0:T(8,128)}, bf16[8,160,512]{2,1,0:T(8,128)(2,1)}, f32[...) custom-call(bf16[10,8,32,384]{3,2,1,0:T(8,128)(2,1)} %alpha_hbm.1, ...), custom_call_target="tpu_custom_call" | custom-call | flops 8999999488 | bytes 29000000 | tf_op jit(solution)/shard_map/pallas_call | solution.py:737
  54.8 9.4 %shard_map.114 = (f32[1,49152]{1,0:T(1,128)}, f32[10,8,32,384]{3,2,1,0:T(8,128)}) custom-call(s32[8]{0:T(128)} %gm_ref.3, bf16[10,8,32,384]{3,2,1,0:T(8,128)(2,1)} %pert_hbm.3, bf16[8,32,384]{2,1,0:T(8,128)(2,1)} %get-tuple-element.9.back_hbm, f32[2,8,32,128]{3,2,1,0:T(8,128)} %get-tuple-element.10.de_hbm, bf16[8,160,512]{2,1,0:T(8,128)(2,1)} %get-tuple-element.11.mt_hbm, ...), custom_call_target="tpu_custom_call" | custom-call | flops 3500000000 | bytes 11000000 | tf_op jit(solution)/shard_map/pallas_call | solution.py:763

commit v7 on v5

--- a/solution.py
+++ b/solution.py
@@ -99,7 +99,7 @@
     whole = [
         pltpu.make_async_copy(a, b, whole_sem.at[i])
         for i, (a, b) in enumerate(
-            [(back_hbm, back_v), (de_hbm, de_v), (pb_hbm, pb_v), (qb_hbm, qb_v), (mt_hbm, mt_v)]
+            [(back_hbm, back_v), (de_hbm, de_v), (pb_hbm, pb_v), (qb_hbm, qb_v)]
         )
     ]
 
@@ -107,6 +107,7 @@
         return [
             pltpu.make_async_copy(pert_hbm.at[:, l], pert_v.at[:, l], in_sem.at[0, l]),
             pltpu.make_async_copy(kk_hbm.at[l], kk_v.at[l], in_sem.at[1, l]),
+            pltpu.make_async_copy(mt_hbm.at[l], mt_v.at[l], in_sem.at[2, l]),
         ]
 
     def store(l):
@@ -316,13 +317,14 @@
                     za[half, l, 16 + HALF * j : 16 + HALF * j + HALF, :] = part[8 : 8 + HALF]
                 za[half, l, 15:16, :] = ytail[l, 0:1, 0:128]
                 za[half, l, 31:32, :] = ytail[l, 1:2, 0:128]
-            for half, l, _z in found:
-
-                @pl.when(2 * l + half != t)
-                def _():
-                    to_tile(za.at[half, l], zr.at[t], sem.at[0], sem.at[1], 2 * l + half).start()
 
         if last == LEVELS // 2:
+
+            @pl.loop(1, TILES)
+            def _(k):
+                s = lax.rem(t + k, TILES)
+                to_tile(za.at[lax.rem(s, 2), s // 2], zr.at[t], sem.at[0], sem.at[1], s).start()
+
             zr[t] = za[core, chip]
 
     def recursion(zr, zo, de, sem):
@@ -771,8 +773,8 @@
             V((LEVELS, ROWS, 128), F32),
             V((LEVELS, COLS, COLS), BF16),
             V(members_shape, F32),
-            dma((5,)),
-            dma((2, LEVELS)),
+            dma((4,)),
+            dma((3, LEVELS)),
             dma((LEVELS,)),
         ],
         compiler_params=pltpu.CompilerParams(vmem_limit_bytes=60 * 1024 * 1024),

time: 63.4 us -> 63 us (level)
  no operation moved by 1% of the time
where the time goes in v7:
time: 63 us; the launch traced here: 62.8 us
  Pallas kernels  62.1 us (99%)
  between operations  0.64 us (1%)
    pallas_call x1, Pallas kernels, shards(): pl.pallas_call(kernel, out_shape=(shape((DROWS, 128), F32), shape((LEVELS...  52.8 us
    pallas_call x1, Pallas kernels, shards(): pl.pallas_call(grad_kernel, out_shape=(shape((1, DROWS * 128), F32), shap...  9.35 us

profile of v7, /device:TPU:1, one launch (start us, length us, event | category | flops | bytes accessed | tf_op | source)
XLA Modules:
  0.0 62.8 jit_solution(15425454019182426143)
XLA Ops:
  0.6 52.8 %shard_map.113 = (f32[384,128]{1,0:T(8,128)}, bf16[8,32,384]{2,1,0:T(8,128)(2,1)}, f32[2,8,32,128]{3,2,1,0:T(8,128)}, bf16[8,160,512]{2,1,0:T(8,128)(2,1)}, f32[...) custom-call(bf16[10,8,32,384]{3,2,1,0:T(8,128)(2,1)} %alpha_hbm.1, ...), custom_call_target="tpu_custom_call" | custom-call | flops 8999999488 | bytes 29000000 | tf_op jit(solution)/shard_map/pallas_call | solution.py:736
  53.4 9.4 %shard_map.114 = (f32[1,49152]{1,0:T(1,128)}, f32[10,8,32,384]{3,2,1,0:T(8,128)}) custom-call(s32[8]{0:T(128)} %gm_ref.3, bf16[10,8,32,384]{3,2,1,0:T(8,128)(2,1)} %pert_hbm.3, bf16[8,32,384]{2,1,0:T(8,128)(2,1)} %get-tuple-element.9.back_hbm, f32[2,8,32,128]{3,2,1,0:T(8,128)} %get-tuple-element.10.de_hbm, bf16[8,160,512]{2,1,0:T(8,128)(2,1)} %get-tuple-element.11.mt_hbm, ...), custom_call_target="tpu_custom_call" | custom-call | flops 3500000000 | bytes 11000000 | tf_op jit(solution)/shard_map/pallas_call | solution.py:762

commit v8 on v7

--- a/solution.py
+++ b/solution.py
@@ -206,13 +206,16 @@
     def w_load(s):
         return pltpu.make_async_copy(w_hbm.at[0, s], w_v.at[s], w_sem.at[s])
 
-    for c in loads:
+    def w_tile(i):
+        late = i // CHIPS
+        return 2 * chip_peer(i - CHIPS * late + 1) + 1 - core + late * (2 * core - 1)
+
+    for c in loads[:4]:
         c.start()
 
-    @pl.loop(0, TILES)
+    @pl.loop(0, CHIPS // 2)
     def _(i):
-        late = i // CHIPS
-        w_load(2 * chip_peer(i - CHIPS * late + 1) + 1 - core + late * (2 * core - 1)).start()
+        w_load(w_tile(i)).start()
 
     barrier = pltpu.get_barrier_semaphore()
 
@@ -290,6 +293,11 @@
         cot_v[pl.ds(pl.multiple_of(16 * i, 16), 16), :] = jnp.concatenate(rows, axis=0).astype(BF16)
 
     loads[0].wait()
+
+    @pl.loop(CHIPS // 2, CHIPS)
+    def _(i):
+        w_load(w_tile(i)).start()
+
     pl.semaphore_wait(barrier, TILES - 1 + LEVELS - 1)
 
     def alpha_of(l, half):
@@ -479,6 +487,16 @@
         tiles = [2 * ch + 1 - core + late * (2 * core - 1) for ch in chips]
         for s in tiles:
             w_load(s).wait()
+
+        @pl.when(late == 0)
+        def _():
+            for i in range(GROUP):
+                w_load(w_tile(CHIPS + GROUP * j + i)).start()
+
+        @pl.when(j == steps // 2)
+        def _():
+            loads[4].start()
+
         for ch, r in zip(chips, back_terms(tiles)):
             sf[late, ch] = r
 

time: 63 us -> 62.8 us (level)
  no operation moved by 1% of the time
where the time goes in v8:
time: 62.8 us; the launch traced here: 62.6 us
  Pallas kernels  62 us (99%)
  between operations  0.64 us (1%)
    pallas_call x1, Pallas kernels, shards(): pl.pallas_call(kernel, out_shape=(shape((DROWS, 128), F32), shape((LEVELS...  52.6 us
    pallas_call x1, Pallas kernels, shards(): pl.pallas_call(grad_kernel, out_shape=(shape((1, DROWS * 128), F32), shap...  9.35 us

profile of v8, /device:TPU:1, one launch (start us, length us, event | category | flops | bytes accessed | tf_op | source)
XLA Modules:
  0.0 62.6 jit_solution(11838350911273972837)
XLA Ops:
  0.6 52.6 %shard_map.113 = (f32[384,128]{1,0:T(8,128)}, bf16[8,32,384]{2,1,0:T(8,128)(2,1)}, f32[2,8,32,128]{3,2,1,0:T(8,128)}, bf16[8,160,512]{2,1,0:T(8,128)(2,1)}, f32[...) custom-call(bf16[10,8,32,384]{3,2,1,0:T(8,128)(2,1)} %alpha_hbm.1, ...), custom_call_target="tpu_custom_call" | custom-call | flops 8999999488 | bytes 29000000 | tf_op jit(solution)/shard_map/pallas_call | solution.py:754
  53.3 9.4 %shard_map.114 = (f32[1,49152]{1,0:T(1,128)}, f32[10,8,32,384]{3,2,1,0:T(8,128)}) custom-call(s32[8]{0:T(128)} %gm_ref.3, bf16[10,8,32,384]{3,2,1,0:T(8,128)(2,1)} %pert_hbm.3, bf16[8,32,384]{2,1,0:T(8,128)(2,1)} %get-tuple-element.9.back_hbm, f32[2,8,32,128]{3,2,1,0:T(8,128)} %get-tuple-element.10.de_hbm, bf16[8,160,512]{2,1,0:T(8,128)(2,1)} %get-tuple-element.11.mt_hbm, ...), custom_call_target="tpu_custom_call" | custom-call | flops 3500000000 | bytes 11000000 | tf_op jit(solution)/shard_map/pallas_call | solution.py:780

commit v9 on v8

--- a/solution.py
+++ b/solution.py
@@ -292,6 +292,17 @@
         ]
         cot_v[pl.ds(pl.multiple_of(16 * i, 16), 16), :] = jnp.concatenate(rows, axis=0).astype(BF16)
 
+    slot_id = lax.broadcasted_iota(jnp.int32, (SLOTS, 128), 0)
+    loads[2].wait()
+    loads[3].wait()
+    turned = jnp.transpose(
+        jnp.concatenate([src_v[...], dst_v[...], jnp.zeros((96, SLOTS), jnp.int32)], axis=0).astype(F32)
+    ).astype(jnp.int32)
+    for s in range(TILES):
+        scol = jnp.broadcast_to(turned[:, s : s + 1], (SLOTS, 128))
+        scol_v[s] = jnp.where(slot_id < pc_ref[t, s], scol, -1)
+        dcol_v[s] = jnp.broadcast_to(turned[:, TILES + s : TILES + s + 1], (SLOTS, 128))
+
     loads[0].wait()
 
     @pl.loop(CHIPS // 2, CHIPS)
@@ -367,7 +378,6 @@
     lane1 = lax.broadcasted_iota(jnp.int32, (1, 128), 1)
     lane = lax.broadcasted_iota(jnp.int32, (SLOTS, 128), 1)
     lgroup = lane >> 5
-    slot_id = lax.broadcasted_iota(jnp.int32, (SLOTS, 128), 0)
     r16 = lax.broadcasted_iota(jnp.int32, (16, 128), 0) - (
         lax.broadcasted_iota(jnp.int32, (16, 128), 1) >> 5
     )
@@ -461,16 +471,6 @@
             puts.append(one_hot(sub384 == target_row(s)))
         both = dot(jnp.concatenate(puts, axis=1), jnp.concatenate(sums, axis=0))
         return both[:, 0:128] + both[:, 128:256]
-
-    loads[2].wait()
-    loads[3].wait()
-    turned = jnp.transpose(
-        jnp.concatenate([src_v[...], dst_v[...], jnp.zeros((96, SLOTS), jnp.int32)], axis=0).astype(F32)
-    ).astype(jnp.int32)
-    for s in range(TILES):
-        scol = jnp.broadcast_to(turned[:, s : s + 1], (SLOTS, 128))
-        scol_v[s] = jnp.where(slot_id < pc_ref[t, s], scol, -1)
-        dcol_v[s] = jnp.broadcast_to(turned[:, TILES + s : TILES + s + 1], (SLOTS, 128))
 
     def off_chip(ch):
         return to_tile(ss.at[ch], sr.at[chip], ss_s, ss_r, tile_of(ch))

time: 62.8 us -> 62.8 us (level)
  no operation moved by 1% of the time
where the time goes in v9:
time: 62.8 us; the launch traced here: 62.6 us
  Pallas kernels  62 us (99%)
  between operations  0.64 us (1%)
    pallas_call x1, Pallas kernels, shards(): pl.pallas_call(kernel, out_shape=(shape((DROWS, 128), F32), shape((LEVELS...  52.6 us
    pallas_call x1, Pallas kernels, shards(): pl.pallas_call(grad_kernel, out_shape=(shape((1, DROWS * 128), F32), shap...  9.36 us

profile of v9, /device:TPU:1, one launch (start us, length us, event | category | flops | bytes accessed | tf_op | source)
XLA Modules:
  0.0 62.6 jit_solution(834795116683432948)
XLA Ops:
  0.6 52.6 %shard_map.113 = (f32[384,128]{1,0:T(8,128)}, bf16[8,32,384]{2,1,0:T(8,128)(2,1)}, f32[2,8,32,128]{3,2,1,0:T(8,128)}, bf16[8,160,512]{2,1,0:T(8,128)(2,1)}, f32[...) custom-call(bf16[10,8,32,384]{3,2,1,0:T(8,128)(2,1)} %alpha_hbm.1, ...), custom_call_target="tpu_custom_call" | custom-call | flops 8999999488 | bytes 29000000 | tf_op jit(solution)/shard_map/pallas_call | solution.py:754
  53.2 9.4 %shard_map.114 = (f32[1,49152]{1,0:T(1,128)}, f32[10,8,32,384]{3,2,1,0:T(8,128)}) custom-call(s32[8]{0:T(128)} %gm_ref.3, bf16[10,8,32,384]{3,2,1,0:T(8,128)(2,1)} %pert_hbm.3, bf16[8,32,384]{2,1,0:T(8,128)(2,1)} %get-tuple-element.9.back_hbm, f32[2,8,32,128]{3,2,1,0:T(8,128)} %get-tuple-element.10.de_hbm, bf16[8,160,512]{2,1,0:T(8,128)(2,1)} %get-tuple-element.11.mt_hbm, ...), custom_call_target="tpu_custom_call" | custom-call | flops 3500000000 | bytes 11000000 | tf_op jit(solution)/shard_map/pallas_call | solution.py:780
